TPU v7x, 256 devices: a whole 4x4x8 slice. The times are simulated.
256 devices in a mesh: gx: 32 (over x, z_hi, y), gy: 8 (over z_lo, core).
Axes of the slice: x: 4, y: 4, z: 8 (z_hi: 2, z_lo: 4; z = z_hi * 4 + z_lo), core: 2. Of those that a mesh axis runs over, the one named last changes fastest.
Arguments:
- moisture_ratio: float32 [1024, 512, 128], P('gx', 'gy'), may hold values from 9 to 12
- kelvin_warmth: float32 [1024, 512, 128], P('gx', 'gy'), may hold values from 284 to 292
- wind_ratio_east: float32 [1024, 512, 128], P('gx', 'gy'), may hold values from 0.05 to 0.35
- wind_ratio_north: float32 [1024, 512, 128], P('gx', 'gy'), may hold values from 0.05 to 0.35
- parcel_particles: float32 [524288, 3, 128], P(('gx', 'gy')), as said below
- parcel_home_region: int32 [524288], P(('gx', 'gy')), may hold values from 0 to 4095
- leaving_parcel_places: int32 [32, 8, 8, 64], P('gx', 'gy'), may hold values from 0 to 2047, as said below
- sending_tallies: int32 [32, 8, 8], P('gx', 'gy'), may hold values from 0 to 64, as said below
Outputs:
- moisture_ratio_later: float32 [1024, 512, 128], P('gx', 'gy')
- kelvin_warmth_later: float32 [1024, 512, 128], P('gx', 'gy')
- droplets_out: float32 [524288, 3, 128], P(('gx', 'gy'))
- incoming_parcels: float32 [32, 8, 8, 64, 3, 128], P('gx', 'gy')
Inputs may be any that keep to these rules, and one draw needn't show every extreme that they name: `leaving_parcel_places`: on each device the 512 entries are distinct local droplet-block indices. `sending_tallies`: each device has one direction with exactly 64 live slots. `parcel_particles`: radius 1 to 15, multiplicity 1 to 10, solute 0.1 to 1.
All inputs are finite; a program needn't handle non-finite values.
Results may differ from a plain program's by a relative error of at most 0.0003.
Values sent between devices are 32-bit elements; how exact they have to be, the bound alone decides.
No kernel may reach another device: no remote copies, remote signals or barrier semaphores. Data moves between devices by JAX's collectives and lax.ppermute only.
A program may use at most 128 MiB of HBM per device.

v0:
```python
import jax
import jax.numpy as jnp
from jax import lax
from jax.experimental import pallas as pl
from jax.experimental.pallas import tpu as pltpu
from jax.sharding import PartitionSpec as P

CX, CY, LEV = 32, 64, 128
ROWS = CX * CY
NB = 2048
SLOTS = 64
CHUNKS = 8
CROWS = ROWS // CHUNKS
LANES_ACC = 4
F32 = jnp.float32
ANY = pl.BlockSpec(memory_space=pltpu.HBM)
VM = pl.BlockSpec(memory_space=pltpu.VMEM)
SM = pl.BlockSpec(memory_space=pltpu.SMEM)


EAST, WEST, NORTH, SOUTH = (0, 4, 5), (1, 6, 7), (2, 4, 6), (3, 5, 7)


def supersat(q, t):
    return q * jnp.exp(-17.27 * (t - 273.15) / (t - 35.86)) * (1.0 / 3.8) - 1.0


def both_halves(s):
    low = lax.broadcasted_iota(jnp.int32, s.shape, 1) < 64
    turned = pltpu.roll(s, 64, 1)
    return jnp.where(low, s, turned), jnp.where(low, turned, s)


def growth_base(r, sol):
    inv = 1.0 / r
    return r * r + 20.0 * (sol * (inv * inv * inv) - 0.01 * inv)


def fetch_rows(count, place, pairs, step=8):
    def group(g, _):
        slots = [g * step + u for u in range(step)]
        rows = [place(s) for s in slots]
        values = [[src[pl.ds(row, 1)] for row in rows] for src, _ in pairs]
        for (_, dst), column in zip(pairs, values):
            for s, value in zip(slots, column):
                dst[pl.ds(s, 1)] = value
        return 0

    lax.fori_loop(0, count // step, group, 0)


def odd_x():
    return lax.rem(lax.axis_index("gx"), 2) == 1


def odd_y():
    return lax.rem(lax.axis_index("gy"), 2) == 1


def kernel_edges(q_h, t_h, xa, xb, ya, yb, slabs, tiles, xsem, ysem):
    copies = []
    for f, src in enumerate((q_h, t_h)):
        for side in range(2):
            copies.append(pltpu.make_async_copy(
                src.at[:, pl.ds((CY - 8) * side, 8)], tiles.at[f, side], ysem.at[f, side]))
            copies.append(pltpu.make_async_copy(
                src.at[(CX - 1) * side], slabs.at[f, side], xsem.at[f, side]))
    for c in copies:
        c.start()
    for c in copies:
        c.wait()
    ox, oy = odd_x(), odd_y()
    for f in range(2):
        low, high = slabs[f, 0], slabs[f, 1]
        xa[f] = jnp.where(ox, low, high)
        xb[f] = jnp.where(ox, high, low)
        low, high = tiles[f, 0, :, 0, :], tiles[f, 1, :, 7, :]
        ya[f] = jnp.where(oy, low, high)
        yb[f] = jnp.where(oy, high, low)


def kernel_advect(
    places, q_h, t_h, we_h, wn_h, parts_h,
    aq, at, table, pv, cw, cs, leave,
    qv, tv, wev, wnv, sems, psem,
):
    fields = ((q_h, qv), (t_h, tv), (we_h, wev), (wn_h, wnv))
    copies = [
        [
            pltpu.make_async_copy(
                src.at[pl.ds(k * CROWS, CROWS)], dst.at[pl.ds(k * CROWS, CROWS)], sems.at[f, k]
            )
            for f, (src, dst) in enumerate(fields)
        ]
        for k in range(CHUNKS)
    ]
    for row in copies:
        for c in row:
            c.start()
    pcopies = [pltpu.make_async_copy(parts_h.at[p], pv.at[p], psem.at[p]) for p in range(3)]
    for c in pcopies:
        c.start()
    yi = lax.broadcasted_iota(jnp.int32, (CY, LEV), 0)
    first, last = yi == 0, yi == CY - 1
    kn = jnp.where(last, 0.0, 0.1).astype(F32)

    def slab(x, _):
        r0 = pl.multiple_of(x * CY, CY)
        rw = pl.multiple_of(jnp.maximum(x - 1, 0) * CY, CY)
        re = pl.multiple_of(jnp.minimum(x + 1, CX - 1) * CY, CY)
        here = pl.ds(r0, CY)
        we, wn = wev[here], wnv[here]
        mid = 0.6 - we - wn
        kw = (we + 0.1) * jnp.where(x > 0, 1.0, 0.0)
        ks = jnp.where(first, 0.0, wn + 0.1)
        ke = jnp.where(x < CX - 1, 0.1, 0.0)

        def carried(v):
            f = v[here]
            return (
                mid * f
                + kw * v[pl.ds(rw, CY)]
                + ks * pltpu.roll(f, 1, 0)
                + ke * v[pl.ds(re, CY)]
                + kn * pltpu.roll(f, CY - 1, 0)
            )

        q, t = carried(qv), carried(tv)
        aq[here] = q
        at[here] = t
        even, odd = both_halves(supersat(q, t))
        table[pl.ds(2 * r0, CY, stride=2)] = even
        table[pl.ds(2 * r0 + 1, CY, stride=2)] = odd
        return 0

    per = CX // CHUNKS
    for k in range(CHUNKS):
        if k == 0:
            copies[0][0].wait()
            copies[0][1].wait()
        copies[k][2].wait()
        copies[k][3].wait()
        if k + 1 < CHUNKS:
            copies[k + 1][0].wait()
            copies[k + 1][1].wait()
        lax.fori_loop(k * per, (k + 1) * per, slab, 0)
    cw[...] = wev[0:CY] + 0.1
    cs[...] = wnv[pl.ds(0, CX, stride=CY)] + 0.1
    for c in pcopies:
        c.wait()
    for d in (0, 4, 5, 1, 6, 7):
        fetch_rows(
            SLOTS, lambda s, d=d: places[0, 0, d, s], [(pv.at[p], leave.at[d, p]) for p in range(3)]
        )


def kernel_fix(
    places, tallies, home, hxa, hxb, hya, hyb, cw, cs, leave, aq_in, at_in, table_in,
    aq, at, table, send_a, send_b, got,
):
    ox, oy = odd_x(), odd_y()
    for f, a in ((0, aq), (1, at)):
        a[0:CY] += cw[...] * jnp.where(ox, hxa[f], hxb[f])
        a[ROWS - CY : ROWS] += 0.1 * jnp.where(ox, hxb[f], hxa[f])
        a[pl.ds(0, CX, stride=CY)] += cs[...] * jnp.where(oy, hya[f], hyb[f])
        a[pl.ds(CY - 1, CX, stride=CY)] += 0.1 * jnp.where(oy, hyb[f], hya[f])

    def refresh(rows, start, count, stride):
        even, odd = both_halves(supersat(aq[rows], at[rows]))
        table[pl.ds(2 * start, count, stride=2 * stride)] = even
        table[pl.ds(2 * start + 1, count, stride=2 * stride)] = odd

    refresh(pl.ds(0, CY), 0, CY, 1)
    refresh(pl.ds(ROWS - CY, CY), ROWS - CY, CY, 1)
    refresh(pl.ds(0, CX, stride=CY), 0, CX, CY)
    refresh(pl.ds(CY - 1, CX, stride=CY), CY - 1, CX, CY)
    slot = lax.broadcasted_iota(jnp.int32, (SLOTS, LEV), 0)
    for send, odd in ((send_a, ox), (send_b, jnp.logical_not(ox))):
        for n in range(3):
            d = jnp.where(odd, WEST[n], EAST[n])
            fetch_rows(SLOTS, lambda s, d=d: home[places[0, 0, d, s]], [(table, got)])
            live = slot < tallies[0, 0, d]
            square = growth_base(leave[d, 0], leave[d, 2]) + 20.0 * got[...]
            send[n, 0] = jnp.where(live, jnp.sqrt(jnp.maximum(square, 0.25)), 0.0)
            send[n, 1] = jnp.where(live, leave[d, 1], 0.0)
            send[n, 2] = jnp.where(live, leave[d, 2], 0.0)


def kernel_grow(places, tallies, home, table, pv, parts_out, cond, ahead, got, new_r, sems, psem):
    copies = [pltpu.make_async_copy(pv.at[p], parts_out.at[p], psem.at[p]) for p in (1, 2)]
    for c in copies:
        c.start()
    outs = []
    per = NB // CHUNKS
    for k in range(CHUNKS):
        fetch_rows(per, lambda s, k=k: home[k * per + s], [(table, got.at[k % 2])], 16)

        def grow(g, _, k=k):
            here = pl.ds(pl.multiple_of(g * 64, 64), 64)
            rows = pl.ds(pl.multiple_of(k * per + g * 64, 64), 64)
            r, m = pv[0, rows], pv[1, rows]
            square = growth_base(r, pv[2, rows]) + 20.0 * got[k % 2, here]
            square = jnp.maximum(square, 0.25)
            new = jnp.sqrt(square)
            new_r[rows] = new
            cond[rows] = (0.0003 * m) * (square * new - r * r * r)
            return 0

        lax.fori_loop(0, per // 64, grow, 0)
        c = pltpu.make_async_copy(
            new_r.at[pl.ds(k * per, per)], parts_out.at[0, pl.ds(k * per, per)], sems.at[k]
        )
        c.start()
        outs.append(c)
    slot = lax.broadcasted_iota(jnp.int32, (SLOTS, LEV), 0)
    for n, d in enumerate((2, 3)):
        fetch_rows(
            SLOTS,
            lambda s, d=d: places[0, 0, d, s],
            [(new_r, ahead.at[n, 0]), (pv.at[1], ahead.at[n, 1]), (pv.at[2], ahead.at[n, 2])],
        )
        live = slot < tallies[0, 0, d]
        for p in range(3):
            ahead[n, p] = jnp.where(live, ahead[n, p], 0.0)
    for c in outs + copies:
        c.wait()


def kernel_forward(ahead, xa, xb, ya, yb):
    ox, oy = odd_x(), odd_y()
    for n in range(3):
        for p in range(3):
            if n == 0:
                up, down = ahead[0, p], ahead[1, p]
            else:
                one, two = (xa, xb) if n == 1 else (xb, xa)
                up = jnp.where(ox, one[1, p], two[1, p])
                down = jnp.where(ox, one[2, p], two[2, p])
            ya[n, p] = jnp.where(oy, down, up)
            yb[n, p] = jnp.where(oy, up, down)


def kernel_deposit(home, cond, aq, at, q_out, t_out, acc, qo, to, sems):
    def clear(g, _):
        for k in range(LANES_ACC):
            acc[k, pl.ds(pl.multiple_of(g * 128, 128), 128)] = jnp.zeros((128, LEV), F32)
        return 0

    lax.fori_loop(0, 2 * ROWS // 128, clear, 0)

    def scatter(g, _):
        b0 = g * LANES_ACC
        at_rows = [home[b0 + k] for k in range(LANES_ACC)]
        sums = [acc[k, pl.ds(at_rows[k], 1)] + cond[pl.ds(b0 + k, 1)] for k in range(LANES_ACC)]
        for k in range(LANES_ACC):
            acc[k, pl.ds(at_rows[k], 1)] = sums[k]
        return 0

    lax.fori_loop(0, NB // LANES_ACC, scatter, 0, unroll=4)
    low = lax.broadcasted_iota(jnp.int32, (64, LEV), 1) < 64
    outs = []
    for j in range(CHUNKS):

        def gather(g, _, j=j):
            r0 = pl.multiple_of(j * CROWS + g * 64, 64)
            rows = pl.ds(r0, 64)
            even, odd = pl.ds(2 * r0, 64, stride=2), pl.ds(2 * r0 + 1, 64, stride=2)
            x0, x1 = acc[0, even], acc[0, odd]
            for k in range(1, LANES_ACC):
                x0, x1 = x0 + acc[k, even], x1 + acc[k, odd]
            dep = jnp.where(low, x0, x1) + pltpu.roll(jnp.where(low, x1, x0), 64, 1)
            qo[rows] = aq[rows] - dep
            to[rows] = at[rows] + 2.5 * dep
            return 0

        lax.fori_loop(0, CROWS // 64, gather, 0)
        for n, (src, dst) in enumerate(((qo, q_out), (to, t_out))):
            rows = pl.ds(j * CROWS, CROWS)
            c = pltpu.make_async_copy(src.at[rows], dst.at[rows], sems.at[n, j])
            c.start()
            outs.append(c)
    for c in outs:
        c.wait()


def kernel_arrive(xa, xb, ya, yb, out, buf, sems):
    ox, oy = odd_x(), odd_y()
    sources = {0: (xa, xb, 0, ox), 1: (xb, xa, 0, ox)}
    for n in range(3):
        sources[NORTH[n]] = (ya, yb, n, oy)
        sources[SOUTH[n]] = (yb, ya, n, oy)
    copies = []
    for d, (one, two, n, odd) in sources.items():
        buf[d] = jnp.where(odd, one[n], two[n])
        copies.append(pltpu.make_async_copy(buf.at[d], out.at[d], sems.at[d]))
        copies[-1].start()
    for c in copies:
        c.wait()


def vmem(*shape):
    return pltpu.VMEM(shape, F32)


def hbm(*shape):
    return pltpu.HBM(shape, F32)


def in_hbm(x):
    return pltpu.with_memory_space_constraint(x, pltpu.HBM)


def dma(*shape):
    return pltpu.SemaphoreType.DMA(shape)


def call(kernel, name, us, ins, outs, shapes, scratch, aliases=None, mib=24):
    return pl.pallas_call(
        kernel,
        in_specs=ins,
        out_specs=outs,
        out_shape=shapes,
        scratch_shapes=scratch,
        input_output_aliases=aliases or {},
        compiler_params=pltpu.CompilerParams(vmem_limit_bytes=mib << 20),
        cost_estimate=pl.CostEstimate(flops=0, bytes_accessed=int(us * 3.0e6), transcendentals=0),
        name=name,
    )


def swapped(value, axis, phase):
    count = lax.axis_size(axis)
    step = [1 if (i + phase) % 2 == 0 else -1 for i in range(count)]
    return lax.ppermute(value, axis, [(i, (i + step[i]) % count) for i in range(count)])


def body(q, t, we, wn, parts, home, places, tallies):
    parts = in_hbm(parts.transpose(1, 0, 2))
    pay = vmem(3, 3, SLOTS, LEV)
    xa, xb, ya, yb = call(
        kernel_edges, "edge_columns", 1, [ANY] * 2, [VM] * 4,
        [vmem(2, CY, LEV)] * 2 + [vmem(2, CX, LEV)] * 2,
        [vmem(2, 2, CY, LEV), vmem(2, 2, CX, 8, LEV), dma(2, 2), dma(2, 2)],
    )(in_hbm(q), in_hbm(t))
    hxb = swapped(xb, "gx", 1)
    hxa = swapped(xa, "gx", 0)
    hyb = swapped(yb, "gy", 1)
    hya = swapped(ya, "gy", 0)
    flat = [in_hbm(x.reshape(ROWS, LEV)) for x in (q, t, we, wn)]
    cells, table_of = vmem(ROWS, LEV), vmem(2 * ROWS, LEV)
    aq, at, table, pv, cw, cs, leave = call(
        kernel_advect, "advect", 5, [SM] + [ANY] * 5, [VM] * 7,
        [cells, cells, table_of, vmem(3, NB, LEV), vmem(CY, LEV), vmem(CX, LEV), vmem(8, 3, SLOTS, LEV)],
        [cells] * 4 + [dma(4, CHUNKS), dma(3)],
    )(places, *flat, parts)
    aq, at, table, sa, sb = call(
        kernel_fix, "fix_edges", 1, [SM] * 3 + [VM] * 10, [VM] * 5,
        [cells, cells, table_of, pay, pay], [vmem(SLOTS, LEV)], {10: 0, 11: 1, 12: 2},
    )(places, tallies, home, hxa, hxb, hya, hyb, cw, cs, leave, aq, at, table)
    gxb = swapped(sb, "gx", 1)
    gxa = swapped(sa, "gx", 0)
    parts_out, cond, ahead = call(
        kernel_grow, "grow", 6, [SM] * 3 + [VM] * 2, [ANY, VM, VM],
        [hbm(3, NB, LEV), vmem(NB, LEV), vmem(2, 3, SLOTS, LEV)],
        [vmem(2, NB // CHUNKS, LEV), vmem(NB, LEV), dma(CHUNKS), dma(2 + 1)],
    )(places, tallies, home, table, pv)
    ya, yb = call(kernel_forward, "forward", 1, [VM] * 3, [VM] * 2, [pay, pay], [])(ahead, gxa, gxb)
    gyb = swapped(yb, "gy", 1)
    gya = swapped(ya, "gy", 0)
    q_out, t_out = call(
        kernel_deposit, "deposit", 6, [SM] + [VM] * 3, [ANY, ANY],
        [hbm(ROWS, LEV), hbm(ROWS, LEV)],
        [vmem(LANES_ACC, 2 * ROWS, LEV), cells, cells, dma(2, CHUNKS)],
    )(home, cond, aq, at)
    arrived = call(
        kernel_arrive, "arrive", 1, [VM] * 4, ANY, hbm(8, 3, SLOTS, LEV),
        [vmem(8, 3, SLOTS, LEV), dma(8)],
    )(gxa, gxb, gya, gyb)
    incoming = arrived.transpose(0, 2, 1, 3)[None, None]
    shape = (CX, CY, LEV)
    return q_out.reshape(shape), t_out.reshape(shape), parts_out.transpose(1, 0, 2), incoming


def solution(mesh):
    cells = P("gx", "gy", None)
    blocks = P(("gx", "gy"), None, None)
    return jax.shard_map(
        body,
        mesh=mesh,
        in_specs=(cells, cells, cells, cells, blocks, P(("gx", "gy")),
                  P("gx", "gy", None, None), P("gx", "gy", None)),
        out_specs=(cells, cells, blocks, P("gx", "gy", None, None, None, None)),
        check_vma=False,
    )
```

profile of v0, /device:TPU:1, one launch (start us, length us, event | category | flops | bytes accessed | tf_op | source)
XLA Modules:
  0.0 61.5 jit_solution(2977301328571269937)
XLA Ops:
  0.6 1.3 %edge_columns.1 = (f32[2,64,128]{2,1,0:T(8,128)S(1)}, f32[2,64,128]{2,1,0:T(8,128)S(1)}, f32[2,32,128]{2,1,0:T(8,128)S(1)}, f32[2,32,128]{2,1,0:T(8,128)S(1)}) custom-call(f32[32,64,128]{2,1,0:T(8,128)} %q_h.1, f32[32,64,128]{2,1,0:T(8,128)} %t_h.1), custom_call_target="tpu_custom_call" | custom-call | bytes 3000000 | tf_op jit(solution)/shard_map/edge_columns/pallas_call | solution.py:340
  1.9 2.2 %collective-permute-start = (f32[2,64,128]{2,1,0:T(8,128)S(1)}, f32[2,64,128]{2,1,0:T(8,128)S(1)}, u32[]{:S(2)}, u32[]{:S(2)}) collective-permute-start(f32[2,64,128]{2,1,0:T(8,128)S(1)} %get-tuple-element.27), channel_id=1, source_target_pairs={{0,8},{8,0},{16,24},{24,16},{32,40},{40,32},{48,56},{56,48},{64,72... | collective-permute-start | bytes 196616 | tf_op jit(solution)/shard_map/ppermute | solution.py:334
  4.1 10.7 %collective-permute-start.1 = (f32[2,64,128]{2,1,0:T(8,128)S(1)}, f32[2,64,128]{2,1,0:T(8,128)S(1)}, u32[]{:S(2)}, u32[]{:S(2)}) collective-permute-start(f32[2,64,128]{2,1,0:T(8,128)S(1)} %get-tuple-element.28), channel_id=1, source_target_pairs={{0,248},{8,16},{16,8},{24,32},{32,24},{40,48},{48,40},{56,64},{64,... | collective-permute-start | bytes 196616 | tf_op jit(solution)/shard_map/ppermute | solution.py:334
  14.9 1.2 %collective-permute-start.2 = (f32[2,32,128]{2,1,0:T(8,128)S(1)}, f32[2,32,128]{2,1,0:T(8,128)S(1)}, u32[]{:S(2)}, u32[]{:S(2)}) collective-permute-start(f32[2,32,128]{2,1,0:T(8,128)S(1)} %get-tuple-element.29), channel_id=1, source_target_pairs={{0,1},{1,0},{2,3},{3,2},{4,5},{5,4},{6,7},{7,6},{8,9},{9,8},{10,11... | collective-permute-start | bytes 98312 | tf_op jit(solution)/shard_map/ppermute | solution.py:334
  16.1 0.6 %collective-permute-start.3 = (f32[2,32,128]{2,1,0:T(8,128)S(1)}, f32[2,32,128]{2,1,0:T(8,128)S(1)}, u32[]{:S(2)}, u32[]{:S(2)}) collective-permute-start(f32[2,32,128]{2,1,0:T(8,128)S(1)} %get-tuple-element.30), channel_id=1, source_target_pairs={{0,7},{1,2},{2,1},{3,4},{4,3},{5,6},{6,5},{7,0},{8,15},{9,10},{10,... | collective-permute-start | bytes 98312 | tf_op jit(solution)/shard_map/ppermute | solution.py:334
  16.7 0.7 %copy-done.1 = s32[1,1,8,64]{3,2,1,0:T(8,128)S(1)} copy-done((s32[1,1,8,64]{3,2,1,0:T(8,128)S(1)}, s32[1,1,8,64]{3,2,1,0:T(8,128)}, u32[]{:S(2)}) %copy-start.1) | copy-done | bytes 2072
  17.4 7.4 %advect.1 = (f32[2048,128]{1,0:T(8,128)S(1)}, f32[2048,128]{1,0:T(8,128)S(1)}, f32[4096,128]{1,0:T(8,128)S(1)}, f32[3,2048,128]{2,1,0:T(8,128)S(1)}, f32[64,128]...) custom-call(s32[1,1,8,64]{3,2,1,0:T(8,128)S(1)} %copy-done.1, f32[2048,128]{1,0:T(8,128)} %bitcast.11, ...), custom_call_target="tpu_custom_call" | custom-call | bytes 15000000 | tf_op jit(solution)/shard_map/advect/pallas_call | solution.py:351
  24.8 0.0 collective-permute-done.2.hya
  24.8 0.0 collective-permute-done.3.hyb
  24.9 0.0 collective-permute-done.hxa
  24.9 0.0 collective-permute-done.1.hxb
  24.9 2.4 %fix_edges.1 = (f32[2048,128]{1,0:T(8,128)S(1)}, f32[2048,128]{1,0:T(8,128)S(1)}, f32[4096,128]{1,0:T(8,128)S(1)}, f32[3,3,64,128]{3,2,1,0:T(8,128)S(1)}, f32[3,3,64,128]{3,2,1,0:T(8,128)S(1)}) custom-call(s32[1,1,8,64]{3,2,1,0:T(8,128)S(1)} %copy-done.1, s32[1,1,8]{2,1,0:T(1,128)S(1)} %copy-done.2, ...), custom_call_target="tpu_custom_call", output_to_operand_aliasing={{0}: (10, {}), {1}: (11, {}), {2}: (12, {})} | custom-call | bytes 3000000 | tf_op jit(solution)/shard_map/fix_edges/pallas_call | solution.py:356
  27.4 0.1 collective-permute-start.4
  27.5 1.3 %collective-permute-start.5 = (f32[3,3,64,128]{3,2,1,0:T(8,128)S(1)}, f32[3,3,64,128]{3,2,1,0:T(8,128)S(1)}, u32[]{:S(2)}, u32[]{:S(2)}) collective-permute-start(f32[3,3,64,128]{3,2,1,0:T(8,128)S(1)} %get-tuple-element.46), channel_id=1, source_target_pairs={{0,248},{8,16},{16,8},{24,32},{32,24},{40,48},{48,40},{56,64},{64,... | collective-permute-start | bytes 884744 | tf_op jit(solution)/shard_map/ppermute | solution.py:334
  28.8 4.8 %grow.1 = (f32[3,2048,128]{2,1,0:T(8,128)}, f32[2048,128]{1,0:T(8,128)S(1)}, f32[2,3,64,128]{3,2,1,0:T(8,128)S(1)}) custom-call(s32[1,1,8,64]{3,2,1,0:T(8,128)S(1)} %copy-done.1, s32[1,1,8]{2,1,0:T(1,128)S(1)} %copy-done.2, s32[2048]{0:T(1024)S(1)} %copy-done, f32[4096,128]{1,0:T(8,128)S(1)} %get-tuple-element.37.table, f32[3,2048,128]{2,1,0:T(8,128)S(1)} %get-tuple-element.38.pv), custom_call_target="tpu_custom_call" | custom-call | bytes 18000000 | tf_op jit(solution)/shard_map/grow/pallas_call | solution.py:362
  33.6 0.9 %collective-permute-done.4.xa = f32[3,3,64,128]{3,2,1,0:T(8,128)S(1)} collective-permute-done((f32[3,3,64,128]{3,2,1,0:T(8,128)S(1)}, f32[3,3,64,128]{3,2,1,0:T(8,128)S(1)}, u32[]{:S(2)}, u32[]{:S(2)}) %collective-permute-start.4) | collective-permute-done | bytes 294944 | tf_op jit(solution)/shard_map/ppermute | solution.py:334
  34.5 9.3 %collective-permute-done.5.xb = f32[3,3,64,128]{3,2,1,0:T(8,128)S(1)} collective-permute-done((f32[3,3,64,128]{3,2,1,0:T(8,128)S(1)}, f32[3,3,64,128]{3,2,1,0:T(8,128)S(1)}, u32[]{:S(2)}, u32[]{:S(2)}) %collective-permute-start.5) | collective-permute-done | bytes 294944 | tf_op jit(solution)/shard_map/ppermute | solution.py:334
  43.8 0.1 forward.1
  43.9 7.3 %collective-permute-start.6 = (f32[3,3,64,128]{3,2,1,0:T(8,128)S(1)}, f32[3,3,64,128]{3,2,1,0:T(8,128)S(1)}, u32[]{:S(2)}, u32[]{:S(2)}) collective-permute-start(f32[3,3,64,128]{3,2,1,0:T(8,128)S(1)} %get-tuple-element.48), channel_id=1, source_target_pairs={{0,1},{1,0},{2,3},{3,2},{4,5},{5,4},{6,7},{7,6},{8,9},{9,8},{10,11... | collective-permute-start | bytes 884744 | tf_op jit(solution)/shard_map/ppermute | solution.py:334
  51.2 0.0 collective-permute-start.7
  51.2 8.0 %deposit.1 = (f32[2048,128]{1,0:T(8,128)}, f32[2048,128]{1,0:T(8,128)}) custom-call(s32[2048]{0:T(1024)S(1)} %copy-done, f32[2048,128]{1,0:T(8,128)S(1)} %get-tuple-element.39.cond, f32[2048,128]{1,0:T(8,128)S(1)} %get-tuple-element.40.aq, f32[2048,128]{1,0:T(8,128)S(1)} %get-tuple-element.41.at), custom_call_target="tpu_custom_call" | custom-call | bytes 18000000 | tf_op jit(solution)/shard_map/deposit/pallas_call | solution.py:370
  59.2 0.0 collective-permute-done.6.ya
  59.2 1.3 %collective-permute-done.7.yb = f32[3,3,64,128]{3,2,1,0:T(8,128)S(1)} collective-permute-done((f32[3,3,64,128]{3,2,1,0:T(8,128)S(1)}, f32[3,3,64,128]{3,2,1,0:T(8,128)S(1)}, u32[]{:S(2)}, u32[]{:S(2)}) %collective-permute-start.7) | collective-permute-done | bytes 294944 | tf_op jit(solution)/shard_map/ppermute | solution.py:334
  60.5 1.0 %arrive.1 = f32[8,3,64,128]{3,2,1,0:T(8,128)} custom-call(f32[3,3,64,128]{3,2,1,0:T(8,128)S(1)} %collective-permute-done.4.xa, f32[3,3,64,128]{3,2,1,0:T(8,128)S(1)} %collective-permute-done.5.xb, f32[3,3,64,128]{3,2,1,0:T(8,128)S(1)} %collective-permute-done.6.ya, f32[3,3,64,128]{3,2,1,0:T(8,128)S(1)} %collective-permute-done.7.yb), custom_call_target="tpu_custom_call" | custom-call | bytes 3000000 | tf_op jit(solution)/shard_map/arrive/pallas_call | solution.py:375
  (5 shorter events, 0.0 us)
Async XLA Ops:
  1.9 22.9 %collective-permute-start = (f32[2,64,128]{2,1,0:T(8,128)S(1)}, f32[2,64,128]{2,1,0:T(8,128)S(1)}, u32[]{:S(2)}, u32[]{:S(2)}) collective-permute-start(f32[2,64,128]{2,1,0:T(8,128)S(1)} %get-tuple-element.27), channel_id=1, source_target_pairs={{0,8},{8,0},{16,24},{24,16},{32,40},{40,32},{48,56},{56,48},{64,72... | collective-permute-start | bytes 196616 | tf_op jit(solution)/shard_map/ppermute | solution.py:334
  4.1 20.7 %collective-permute-start.1 = (f32[2,64,128]{2,1,0:T(8,128)S(1)}, f32[2,64,128]{2,1,0:T(8,128)S(1)}, u32[]{:S(2)}, u32[]{:S(2)}) collective-permute-start(f32[2,64,128]{2,1,0:T(8,128)S(1)} %get-tuple-element.28), channel_id=1, source_target_pairs={{0,248},{8,16},{16,8},{24,32},{32,24},{40,48},{48,40},{56,64},{64,... | collective-permute-start | bytes 196616 | tf_op jit(solution)/shard_map/ppermute | solution.py:334
  14.9 10.0 %collective-permute-start.2 = (f32[2,32,128]{2,1,0:T(8,128)S(1)}, f32[2,32,128]{2,1,0:T(8,128)S(1)}, u32[]{:S(2)}, u32[]{:S(2)}) collective-permute-start(f32[2,32,128]{2,1,0:T(8,128)S(1)} %get-tuple-element.29), channel_id=1, source_target_pairs={{0,1},{1,0},{2,3},{3,2},{4,5},{5,4},{6,7},{7,6},{8,9},{9,8},{10,11... | collective-permute-start | bytes 98312 | tf_op jit(solution)/shard_map/ppermute | solution.py:334
  16.1 8.7 %collective-permute-start.3 = (f32[2,32,128]{2,1,0:T(8,128)S(1)}, f32[2,32,128]{2,1,0:T(8,128)S(1)}, u32[]{:S(2)}, u32[]{:S(2)}) collective-permute-start(f32[2,32,128]{2,1,0:T(8,128)S(1)} %get-tuple-element.30), channel_id=1, source_target_pairs={{0,7},{1,2},{2,1},{3,4},{4,3},{5,6},{6,5},{7,0},{8,15},{9,10},{10,... | collective-permute-start | bytes 98312 | tf_op jit(solution)/shard_map/ppermute | solution.py:334
  16.7 0.7 %copy-start.1 = (s32[1,1,8,64]{3,2,1,0:T(8,128)S(1)}, s32[1,1,8,64]{3,2,1,0:T(8,128)}, u32[]{:S(2)}) copy-start(s32[1,1,8,64]{3,2,1,0:T(8,128)} %places.5) | copy-start | bytes 6148
  17.4 7.5 %copy-start = (s32[2048]{0:T(1024)S(1)}, s32[2048]{0:T(1024)}, u32[]{:S(2)}) copy-start(s32[2048]{0:T(1024)} %home.5) | copy-start | bytes 24580
  17.4 7.5 %copy-start.2 = (s32[1,1,8]{2,1,0:T(1,128)S(1)}, s32[1,1,8]{2,1,0:T(1,128)}, u32[]{:S(2)}) copy-start(s32[1,1,8]{2,1,0:T(1,128)} %tallies.3) | copy-start | bytes 100
  27.4 7.2 %collective-permute-start.4 = (f32[3,3,64,128]{3,2,1,0:T(8,128)S(1)}, f32[3,3,64,128]{3,2,1,0:T(8,128)S(1)}, u32[]{:S(2)}, u32[]{:S(2)}) collective-permute-start(f32[3,3,64,128]{3,2,1,0:T(8,128)S(1)} %get-tuple-element.45), channel_id=1, source_target_pairs={{0,8},{8,0},{16,24},{24,16},{32,40},{40,32},{48,56},{56,48},{64,72... | collective-permute-start | bytes 884744 | tf_op jit(solution)/shard_map/ppermute | solution.py:334
  27.5 16.3 %collective-permute-start.5 = (f32[3,3,64,128]{3,2,1,0:T(8,128)S(1)}, f32[3,3,64,128]{3,2,1,0:T(8,128)S(1)}, u32[]{:S(2)}, u32[]{:S(2)}) collective-permute-start(f32[3,3,64,128]{3,2,1,0:T(8,128)S(1)} %get-tuple-element.46), channel_id=1, source_target_pairs={{0,248},{8,16},{16,8},{24,32},{32,24},{40,48},{48,40},{56,64},{64,... | collective-permute-start | bytes 884744 | tf_op jit(solution)/shard_map/ppermute | solution.py:334
  43.9 15.3 %collective-permute-start.6 = (f32[3,3,64,128]{3,2,1,0:T(8,128)S(1)}, f32[3,3,64,128]{3,2,1,0:T(8,128)S(1)}, u32[]{:S(2)}, u32[]{:S(2)}) collective-permute-start(f32[3,3,64,128]{3,2,1,0:T(8,128)S(1)} %get-tuple-element.48), channel_id=1, source_target_pairs={{0,1},{1,0},{2,3},{3,2},{4,5},{5,4},{6,7},{7,6},{8,9},{9,8},{10,11... | collective-permute-start | bytes 884744 | tf_op jit(solution)/shard_map/ppermute | solution.py:334
  51.2 9.3 %collective-permute-start.7 = (f32[3,3,64,128]{3,2,1,0:T(8,128)S(1)}, f32[3,3,64,128]{3,2,1,0:T(8,128)S(1)}, u32[]{:S(2)}, u32[]{:S(2)}) collective-permute-start(f32[3,3,64,128]{3,2,1,0:T(8,128)S(1)} %get-tuple-element.49), channel_id=1, source_target_pairs={{0,7},{1,2},{2,1},{3,4},{4,3},{5,6},{6,5},{7,0},{8,15},{9,10},{10,... | collective-permute-start | bytes 884744 | tf_op jit(solution)/shard_map/ppermute | solution.py:334
where the time goes:
time: 61.6 us; the launch traced here: 61.5 us
  Pallas kernels  25 us (41%)
  starting transfers between devices  23.5 us (38%)
  waiting for transfers between devices  11.5 us (19%)
  between operations  0.75 us (1%)
  local copies, waits for them, and re-layouts  0.69 us (1%)
    ppermute x8, starting transfers between devices, swapped(): lax.ppermute(value, axis, [(i, (i + step[i]) % count) for i in range(coun...  23.5 us
    ppermute x8, waiting for transfers between devices, swapped(): lax.ppermute(value, axis, [(i, (i + step[i]) % count) for i in range(coun...  11.5 us
    pallas_call x1, Pallas kernels, body(): call(kernel_deposit, 'deposit', 6, [SM] + [VM] * 3, [ANY, ANY], [hbm(ROWS...  7.96 us
    pallas_call x1, Pallas kernels, body(): call(kernel_advect, 'advect', 5, [SM] + [ANY] * 5, [VM] * 7, [cells, cell...  7.4 us
    pallas_call x1, Pallas kernels, body(): call(kernel_grow, 'grow', 6, [SM] * 3 + [VM] * 2, [ANY, VM, VM], [hbm(3,...  4.83 us
    pallas_call x1, Pallas kernels, body(): call(kernel_fix, 'fix_edges', 1, [SM] * 3 + [VM] * 10, [VM] * 5, [cells,...  2.45 us
    pallas_call x1, Pallas kernels, body(): call(kernel_edges, 'edge_columns', 1, [ANY] * 2, [VM] * 4, [vmem(2, CY, L...  1.3 us
  transfers between devices with their start and end apart: 8, of which 3 were waited for; matrix products, arithmetic and copies ran while one was open for 0% of the time, Pallas kernels for 33%

commit v1 on v0

v1 whole, which is shorter than its diff:
```python
import math

import jax
import jax.numpy as jnp
from jax import lax
from jax.experimental import pallas as pl
from jax.experimental.pallas import tpu as pltpu
from jax.sharding import PartitionSpec as P

CX, CY, LEV = 32, 64, 128
ROWS = CX * CY
NB = 2048
SLOTS = 64
CHUNKS = 8
CROWS = ROWS // CHUNKS
LANES_ACC = 4
UNROLL = 8
POWER = 17.27 * (273.15 - 35.86) * math.log2(math.e)
SHIFT = 17.27 * math.log2(math.e) + math.log2(3.8)
F32 = jnp.float32
ANY = pl.BlockSpec(memory_space=pltpu.HBM)
VM = pl.BlockSpec(memory_space=pltpu.VMEM)
SM = pl.BlockSpec(memory_space=pltpu.SMEM)


EAST, WEST, NORTH, SOUTH = (0, 4, 5), (1, 6, 7), (2, 4, 6), (3, 5, 7)


def supersat(q, t):
    return q * jnp.exp2(POWER / (t - 35.86) - SHIFT) - 1.0


def both_halves(s):
    low = lax.broadcasted_iota(jnp.int32, s.shape, 1) < 64
    turned = pltpu.roll(s, 64, 1)
    return jnp.where(low, s, turned), jnp.where(low, turned, s)


def root(x):
    return x * lax.rsqrt(x)


def growth_base(r, sol):
    inv = 1.0 / r
    return r * r + 20.0 * (sol * (inv * inv * inv) - 0.01 * inv)


def fetch_rows(count, place, pairs, step=64):
    def group(g, _):
        slots = [g * step + u for u in range(step)]
        rows = [place(s) for s in slots]
        values = [[src[pl.ds(row, 1)] for row in rows] for src, _ in pairs]
        for (_, dst), column in zip(pairs, values):
            for s, value in zip(slots, column):
                dst[pl.ds(s, 1)] = value
        return 0

    lax.fori_loop(0, count // step, group, 0)


def odd_x():
    return lax.rem(lax.axis_index("gx"), 2) == 1


def odd_y():
    return lax.rem(lax.axis_index("gy"), 2) == 1


def gx_sends(sends):
    ox = odd_x()
    for send, odd in zip(sends, (jnp.logical_not(ox), ox)):
        for n in range(3):
            yield send, n, jnp.where(odd, WEST[n], EAST[n])


def kernel_send(
    q_h, t_h, places_h, tallies_h, parts_h, xb, xa, yb, ya, rest,
    slabs, tiles, places, tallies, xsem, ysem, sems,
):
    copies = []
    for f, src in enumerate((q_h, t_h)):
        for side in range(2):
            copies.append(pltpu.make_async_copy(
                src.at[:, pl.ds((CY - 8) * side, 8)], tiles.at[f, side], ysem.at[f, side]))
            copies.append(pltpu.make_async_copy(
                src.at[(CX - 1) * side], slabs.at[f, side], xsem.at[f, side]))
    copies.append(pltpu.make_async_copy(places_h, places, sems.at[0]))
    copies.append(pltpu.make_async_copy(tallies_h, tallies, sems.at[1]))
    planes = [pltpu.make_async_copy(parts_h.at[1 + p], rest.at[p], sems.at[2 + p]) for p in range(2)]
    for c in copies + planes:
        c.start()
    for c in copies:
        c.wait()
    ox, oy = odd_x(), odd_y()
    for f in range(2):
        low, high = slabs[f, 0], slabs[f, 1]
        xa[f] = jnp.where(ox, low, high)
        xb[f] = jnp.where(ox, high, low)
        low, high = tiles[f, 0, :, 0, :], tiles[f, 1, :, 7, :]
        ya[f] = jnp.where(oy, low, high)
        yb[f] = jnp.where(oy, high, low)
    slot = lax.broadcasted_iota(jnp.int32, (SLOTS, LEV), 0)
    for p in range(2):
        planes[p].wait()
        for send, n, d in gx_sends((xb, xa)):
            dst = send.at[2 + 2 * n + p]
            fetch_rows(SLOTS, lambda s, d=d: places[0, 0, d, s], [(rest.at[p], dst)])
            dst[...] = jnp.where(slot < tallies[0, 0, d], dst[...], 0.0)


def stencil(fields, sems, outs):
    aq, at, table = outs
    per = CX // CHUNKS
    copies = {
        (f, k): pltpu.make_async_copy(
            src.at[pl.ds(k * CROWS, CROWS)], dst.at[pl.ds(k * CROWS, CROWS)], sems.at[f, k]
        )
        for k in range(CHUNKS)
        for f, (src, dst) in enumerate(fields)
    }
    for c in copies.values():
        c.start()
    (_, qv), (_, tv), (_, wev), (_, wnv) = fields
    yi = lax.broadcasted_iota(jnp.int32, (CY, LEV), 0)
    first, last = yi == 0, yi == CY - 1
    kn = jnp.where(last, 0.0, 0.1).astype(F32)

    def slab(x, _):
        r0 = pl.multiple_of(x * CY, CY)
        rw = pl.multiple_of(jnp.maximum(x - 1, 0) * CY, CY)
        re = pl.multiple_of(jnp.minimum(x + 1, CX - 1) * CY, CY)
        here = pl.ds(r0, CY)
        we, wn = wev[here], wnv[here]
        mid = 0.6 - we - wn
        kw = (we + 0.1) * jnp.where(x > 0, 1.0, 0.0)
        ks = jnp.where(first, 0.0, wn + 0.1)
        ke = jnp.where(x < CX - 1, 0.1, 0.0)

        def carried(v):
            f = v[here]
            return (
                mid * f
                + kw * v[pl.ds(rw, CY)]
                + ks * pltpu.roll(f, 1, 0)
                + ke * v[pl.ds(re, CY)]
                + kn * pltpu.roll(f, CY - 1, 0)
            )

        q, t = carried(qv), carried(tv)
        aq[here] = q
        at[here] = t
        even, odd = both_halves(supersat(q, t))
        table[pl.ds(2 * r0, CY, stride=2)] = even
        table[pl.ds(2 * r0 + 1, CY, stride=2)] = odd
        return 0

    waited = set()

    def wait(*keys):
        for key in keys:
            if key in copies and key not in waited:
                copies[key].wait()
                waited.add(key)

    for k in range(CHUNKS):
        wait(*[(f, j) for j in (k - 1, k, k + 1) for f in range(2)], (2, k), (3, k))
        lax.fori_loop(k * per, (k + 1) * per, slab, 0, unroll=4)


def kernel_advect(
    places_h, q_h, t_h, we_h, wn_h, parts_h,
    aq, at, table, cw, cs, radius, leave_b, leave_a,
    qv, tv, wev, wnv, places, sems, psem,
):
    copies = [
        pltpu.make_async_copy(places_h, places, psem.at[0]),
        pltpu.make_async_copy(parts_h.at[0], radius, psem.at[1]),
    ]
    for c in copies:
        c.start()
    stencil(((q_h, qv), (t_h, tv), (we_h, wev), (wn_h, wnv)), sems, (aq, at, table))
    cw[...] = wev[0:CY] + 0.1
    cs[...] = wnv[pl.ds(0, CX, stride=CY)] + 0.1
    for c in copies:
        c.wait()
    for leave, n, d in gx_sends((leave_b, leave_a)):
        fetch_rows(SLOTS, lambda s, d=d: places[0, 0, d, s], [(radius, leave.at[n])])


def kernel_fix(
    places_h, tallies_h, home_h, hxb, hxa, hyb, hya, cw, cs, leave_b, leave_a, xb, xa, aq_in, at_in, table_in,
    aq, at, table, send_b, send_a, got, places, tallies, home, sems,
):
    lists = ((places_h, places), (tallies_h, tallies), (home_h, home))
    copies = [pltpu.make_async_copy(a, b, sems.at[k]) for k, (a, b) in enumerate(lists)]
    for c in copies:
        c.start()
    ox, oy = odd_x(), odd_y()
    for f, a in ((0, aq), (1, at)):
        a[0:CY] += cw[...] * jnp.where(ox, hxa[f], hxb[f])
        a[ROWS - CY : ROWS] += 0.1 * jnp.where(ox, hxb[f], hxa[f])
        a[pl.ds(0, CX, stride=CY)] += cs[...] * jnp.where(oy, hya[f], hyb[f])
        a[pl.ds(CY - 1, CX, stride=CY)] += 0.1 * jnp.where(oy, hyb[f], hya[f])

    def refresh(rows, start, count, stride):
        even, odd = both_halves(supersat(aq[rows], at[rows]))
        table[pl.ds(2 * start, count, stride=2 * stride)] = even
        table[pl.ds(2 * start + 1, count, stride=2 * stride)] = odd

    refresh(pl.ds(0, CY), 0, CY, 1)
    refresh(pl.ds(ROWS - CY, CY), ROWS - CY, CY, 1)
    refresh(pl.ds(0, CX, stride=CY), 0, CX, CY)
    refresh(pl.ds(CY - 1, CX, stride=CY), CY - 1, CX, CY)
    for c in copies:
        c.wait()
    slot = lax.broadcasted_iota(jnp.int32, (SLOTS, LEV), 0)
    radii, rests = (leave_b, leave_a), (xb, xa)
    for k, (send, n, d) in enumerate(gx_sends((send_b, send_a))):
        fetch_rows(SLOTS, lambda s, d=d: home[places[0, 0, d, s]], [(table, got)])
        square = growth_base(radii[k // 3][n], rests[k // 3][3 + 2 * n]) + 20.0 * got[...]
        send[n] = jnp.where(slot < tallies[0, 0, d], root(jnp.maximum(square, 0.25)), 0.0)


def kernel_grow(places, tallies, home, table, radius, rest, parts_out, cond, ahead, got, new_r, sems, psem):
    copies = [pltpu.make_async_copy(rest.at[p], parts_out.at[1 + p], psem.at[p]) for p in range(2)]
    for c in copies:
        c.start()
    outs = []
    per = NB // CHUNKS
    for k in range(CHUNKS):
        fetch_rows(per, lambda s, k=k: home[k * per + s], [(table, got.at[k % 2])])

        def grow(g, _, k=k):
            here = pl.ds(pl.multiple_of(g * 64, 64), 64)
            rows = pl.ds(pl.multiple_of(k * per + g * 64, 64), 64)
            r, m = radius[rows], rest[0, rows]
            square = growth_base(r, rest[1, rows]) + 20.0 * got[k % 2, here]
            square = jnp.maximum(square, 0.25)
            new = root(square)
            new_r[rows] = new
            taken = (0.0003 * m) * (square * new - r * r * r)
            cond[rows] = taken + pltpu.roll(taken, 64, 1)
            return 0

        lax.fori_loop(0, per // 64, grow, 0, unroll=4)
        c = pltpu.make_async_copy(
            new_r.at[pl.ds(k * per, per)], parts_out.at[0, pl.ds(k * per, per)], sems.at[k]
        )
        c.start()
        outs.append(c)
    slot = lax.broadcasted_iota(jnp.int32, (SLOTS, LEV), 0)
    for n, d in enumerate((2, 3)):
        fetch_rows(
            SLOTS,
            lambda s, d=d: places[0, 0, d, s],
            [(new_r, ahead.at[n, 0]), (rest.at[0], ahead.at[n, 1]), (rest.at[1], ahead.at[n, 2])],
        )
        live = slot < tallies[0, 0, d]
        for p in range(3):
            ahead[n, p] = jnp.where(live, ahead[n, p], 0.0)
    for c in outs + copies:
        c.wait()


def piece(radius, rest, n, p):
    return radius[n] if p == 0 else rest[1 + 2 * n + p]


def kernel_forward(ahead, ra, rb, ma, mb, ya, yb):
    ox, oy = odd_x(), odd_y()
    a, b = (ra, ma), (rb, mb)
    for n in range(3):
        for p in range(3):
            if n == 0:
                up, down = ahead[0, p], ahead[1, p]
            else:
                one, two = (a, b) if n == 1 else (b, a)
                up = jnp.where(ox, piece(*one, 1, p), piece(*two, 1, p))
                down = jnp.where(ox, piece(*one, 2, p), piece(*two, 2, p))
            ya[n, p] = jnp.where(oy, down, up)
            yb[n, p] = jnp.where(oy, up, down)


def kernel_deposit(home, cond, aq, at, q_out, t_out, acc, qo, to, sems):
    def clear(g, _):
        for k in range(LANES_ACC):
            acc[k, pl.ds(pl.multiple_of(g * 128, 128), 128)] = jnp.zeros((128, LEV), F32)
        return 0

    lax.fori_loop(0, ROWS // 128, clear, 0)
    half = lax.broadcasted_iota(jnp.int32, (1, LEV), 1) // 64

    def scatter(g, _):
        b0 = g * LANES_ACC
        where = [home[b0 + k] for k in range(LANES_ACC)]
        rows = [pl.ds(c >> 1, 1) for c in where]
        sums = [
            acc[k, rows[k]] + jnp.where(half == (where[k] & 1), cond[pl.ds(b0 + k, 1)], 0.0)
            for k in range(LANES_ACC)
        ]
        for k in range(LANES_ACC):
            acc[k, rows[k]] = sums[k]
        return 0

    lax.fori_loop(0, NB // LANES_ACC, scatter, 0, unroll=UNROLL)
    outs = []
    for j in range(CHUNKS):

        def gather(g, _, j=j):
            rows = pl.ds(pl.multiple_of(j * CROWS + g * 64, 64), 64)
            dep = acc[0, rows]
            for k in range(1, LANES_ACC):
                dep = dep + acc[k, rows]
            qo[rows] = aq[rows] - dep
            to[rows] = at[rows] + 2.5 * dep
            return 0

        lax.fori_loop(0, CROWS // 64, gather, 0)
        for n, (src, dst) in enumerate(((qo, q_out), (to, t_out))):
            rows = pl.ds(j * CROWS, CROWS)
            c = pltpu.make_async_copy(src.at[rows], dst.at[rows], sems.at[n, j])
            c.start()
            outs.append(c)
    for c in outs:
        c.wait()


def kernel_arrive(ra, rb, ma, mb, ya, yb, out, buf, sems):
    ox, oy = odd_x(), odd_y()
    copies = []

    def ship(d):
        copies.append(pltpu.make_async_copy(buf.at[d], out.at[d], sems.at[d]))
        copies[-1].start()

    for d, one, two in ((0, (ra, ma), (rb, mb)), (1, (rb, mb), (ra, ma))):
        for p in range(3):
            buf[d, p] = jnp.where(ox, piece(*one, 0, p), piece(*two, 0, p))
        ship(d)
    for n in range(3):
        for d, one, two in ((NORTH[n], ya, yb), (SOUTH[n], yb, ya)):
            buf[d] = jnp.where(oy, one[n], two[n])
            ship(d)
    for c in copies:
        c.wait()


def vmem(*shape):
    return pltpu.VMEM(shape, F32)


def hbm(*shape):
    return pltpu.HBM(shape, F32)


def in_hbm(x):
    return pltpu.with_memory_space_constraint(x, pltpu.HBM)


def dma(*shape):
    return pltpu.SemaphoreType.DMA(shape)


def call(kernel, name, us, ins, outs, shapes, scratch, aliases=None, mib=24):
    return pl.pallas_call(
        kernel,
        in_specs=ins,
        out_specs=outs,
        out_shape=shapes,
        scratch_shapes=scratch,
        input_output_aliases=aliases or {},
        compiler_params=pltpu.CompilerParams(vmem_limit_bytes=mib << 20),
        cost_estimate=pl.CostEstimate(flops=0, bytes_accessed=int(us * 3.0e6), transcendentals=0),
        name=name,
    )


def swapped(value, axis, phase):
    count = lax.axis_size(axis)
    step = [1 if (i + phase) % 2 == 0 else -1 for i in range(count)]
    return lax.ppermute(value, axis, [(i, (i + step[i]) % count) for i in range(count)])


def body(q, t, we, wn, parts, home, places, tallies):
    parts = in_hbm(parts.transpose(1, 0, 2))
    q_h, t_h = in_hbm(q), in_hbm(t)
    flat = [in_hbm(x.reshape(ROWS, LEV)) for x in (q, t, we, wn)]
    places_h, tallies_h, home_h = in_hbm(places), in_hbm(tallies), in_hbm(home)
    places_s, tallies_s = pltpu.SMEM((1, 1, 8, SLOTS), jnp.int32), pltpu.SMEM((1, 1, 8), jnp.int32)
    cells, table_of, blocks = vmem(ROWS, LEV), vmem(2 * ROWS, LEV), vmem(NB, LEV)
    pay, radii = vmem(3, 3, SLOTS, LEV), vmem(3, SLOTS, LEV)
    xb, xa, yb, ya, rest = call(
        kernel_send, "send_edges", 1, [ANY] * 5, [VM] * 5,
        [vmem(8, CY, LEV)] * 2 + [vmem(2, CX, LEV)] * 2 + [vmem(2, NB, LEV)],
        [vmem(2, 2, CY, LEV), vmem(2, 2, CX, 8, LEV), places_s, tallies_s, dma(2, 2), dma(2, 2), dma(4)],
    )(q_h, t_h, places_h, tallies_h, parts)
    hxb = swapped(xb, "gx", 1)
    hxa = swapped(xa, "gx", 0)
    hyb = swapped(yb, "gy", 1)
    hya = swapped(ya, "gy", 0)
    aq, at, table, cw, cs, radius, leave_b, leave_a = call(
        kernel_advect, "advect", 6, [ANY] * 6, [VM] * 8,
        [cells, cells, table_of, vmem(CY, LEV), vmem(CX, LEV), blocks, radii, radii],
        [cells] * 4 + [places_s, dma(4, CHUNKS), dma(2)],
    )(places_h, *flat, parts)
    aq, at, table, rb, ra = call(
        kernel_fix, "fix_edges", 1, [ANY] * 3 + [VM] * 13, [VM] * 5,
        [cells, cells, table_of, radii, radii],
        [vmem(SLOTS, LEV), places_s, tallies_s, pltpu.SMEM((NB,), jnp.int32), dma(3)],
        {13: 0, 14: 1, 15: 2},
    )(places_h, tallies_h, home_h, hxb, hxa, hyb, hya, cw, cs, leave_b, leave_a, xb, xa, aq, at, table)
    rb = swapped(rb, "gx", 1)
    ra = swapped(ra, "gx", 0)
    parts_out, cond, ahead = call(
        kernel_grow, "grow", 6, [SM] * 3 + [VM] * 3, [ANY, VM, VM],
        [hbm(3, NB, LEV), blocks, vmem(2, 3, SLOTS, LEV)],
        [vmem(2, NB // CHUNKS, LEV), blocks, dma(CHUNKS), dma(2)],
    )(places, tallies, home, table, radius, rest)
    ya, yb = call(kernel_forward, "forward", 1, [VM] * 5, [VM] * 2, [pay, pay], [])(ahead, ra, rb, hxa, hxb)
    gyb = swapped(yb, "gy", 1)
    gya = swapped(ya, "gy", 0)
    q_out, t_out = call(
        kernel_deposit, "deposit", 6, [SM] + [VM] * 3, [ANY, ANY],
        [hbm(ROWS, LEV), hbm(ROWS, LEV)],
        [vmem(LANES_ACC, ROWS, LEV), cells, cells, dma(2, CHUNKS)],
    )(home, cond, aq, at)
    arrived = call(
        kernel_arrive, "arrive", 1, [VM] * 6, ANY, hbm(8, 3, SLOTS, LEV),
        [vmem(8, 3, SLOTS, LEV), dma(8)],
    )(ra, rb, hxa, hxb, gya, gyb)
    incoming = arrived.transpose(0, 2, 1, 3)[None, None]
    shape = (CX, CY, LEV)
    return q_out.reshape(shape), t_out.reshape(shape), parts_out.transpose(1, 0, 2), incoming


def solution(mesh):
    cells = P("gx", "gy", None)
    blocks = P(("gx", "gy"), None, None)
    return jax.shard_map(
        body,
        mesh=mesh,
        in_specs=(cells, cells, cells, cells, blocks, P(("gx", "gy")),
                  P("gx", "gy", None, None), P("gx", "gy", None)),
        out_specs=(cells, cells, blocks, P("gx", "gy", None, None, None, None)),
        check_vma=False,
    )
```

time: 61.6 us -> 56.9 us (0.924)
  Pallas kernels: 25 us -> 20.1 us
  waiting for transfers between devices: 11.5 us -> 13.3 us
  starting transfers between devices: 23.5 us -> 22.6 us
  local copies, waits for them, and re-layouts: 0.69 us -> 0.02 us
    pallas_call x6, Pallas kernels: 17 us -> 14 us  [the longest x1 4.55 us: body(): call(kernel_grow, 'grow', 6, [SM] * 3 + [VM] * 3, [ANY, VM, VM], [hbm(3,...]
    pallas_call x1, Pallas kernels: 7.96 us -> 6.1 us  [body(): call(kernel_deposit, 'deposit', 6, [SM] + [VM] * 3, [ANY, ANY], [hbm(ROWS...]
    ppermute x8, waiting for transfers between devices: 11.5 us -> 13.3 us  [swapped(): lax.ppermute(value, axis, [(i, (i + step[i]) % count) for i in range(coun...]
    ppermute x8, starting transfers between devices: 23.5 us -> 22.6 us  [swapped(): lax.ppermute(value, axis, [(i, (i + step[i]) % count) for i in range(coun...]
    unnamed x6, local copies, waits for them, and re-layouts: 0.69 us -> 0.02 us
  transfers between devices with their start and end apart: 8 -> 8, of which waited for: 3 -> 3; matrix products, arithmetic and copies ran while one was open for 0% -> 0% of each run, Pallas kernels for 33% -> 26%
where the time goes in v1:
time: 56.9 us; the launch traced here: 56.7 us
  starting transfers between devices  22.6 us (40%)
  Pallas kernels  20.1 us (35%)
  waiting for transfers between devices  13.3 us (23%)
  between operations  0.74 us (1%)
    ppermute x8, starting transfers between devices, swapped(): lax.ppermute(value, axis, [(i, (i + step[i]) % count) for i in range(coun...  22.6 us
    ppermute x8, waiting for transfers between devices, swapped(): lax.ppermute(value, axis, [(i, (i + step[i]) % count) for i in range(coun...  13.3 us
    pallas_call x1, Pallas kernels, body(): call(kernel_deposit, 'deposit', 6, [SM] + [VM] * 3, [ANY, ANY], [hbm(ROWS...  6.1 us
    pallas_call x1, Pallas kernels, body(): call(kernel_grow, 'grow', 6, [SM] * 3 + [VM] * 3, [ANY, VM, VM], [hbm(3,...  4.55 us
    pallas_call x1, Pallas kernels, body(): call(kernel_advect, 'advect', 6, [ANY] * 6, [VM] * 8, [cells, cells, tabl...  3.92 us
    pallas_call x1, Pallas kernels, body(): call(kernel_send, 'send_edges', 1, [ANY] * 5, [VM] * 5, [vmem(8, CY, LEV)...  2.82 us
    pallas_call x1, Pallas kernels, body(): call(kernel_fix, 'fix_edges', 1, [ANY] * 3 + [VM] * 13, [VM] * 5, [cells,...  1.67 us
  transfers between devices with their start and end apart: 8, of which 3 were waited for; matrix products, arithmetic and copies ran while one was open for 0% of the time, Pallas kernels for 26%

profile of v1, /device:TPU:1, one launch (start us, length us, event | category | flops | bytes accessed | tf_op | source)
XLA Modules:
  0.0 56.7 jit_solution(9966359315367207615)
XLA Ops:
  0.6 2.8 %send_edges.1 = (f32[8,64,128]{2,1,0:T(8,128)S(1)}, f32[8,64,128]{2,1,0:T(8,128)S(1)}, f32[2,32,128]{2,1,0:T(8,128)S(1)}, f32[2,32,128]{2,1,0:T(8,128)S(1)}, f32[2,2048,128]{2,1,0:T(8,128)S(1)}) custom-call(f32[32,64,128]{2,1,0:T(8,128)} %q_h.1, f32[32,64,128]{2,1,0:T(8,128)} %t_h.1, s32[1,1,8,64]{3,2,1,0:T(8,128)} %places.1, s32[1,1,8]{2,1,0:T(1,128)} %tallies.1, ...), custom_call_target="tpu_custom_call" | custom-call | bytes 3000000 | tf_op jit(solution)/shard_map/send_edges/pallas_call | solution.py:392
  3.5 12.5 %collective-permute-start = (f32[8,64,128]{2,1,0:T(8,128)S(1)}, f32[8,64,128]{2,1,0:T(8,128)S(1)}, u32[]{:S(2)}, u32[]{:S(2)}) collective-permute-start(f32[8,64,128]{2,1,0:T(8,128)S(1)} %get-tuple-element.29.xb), channel_id=1, source_target_pairs={{0,248},{8,16},{16,8},{24,32},{32,24},{40,48},{48,40},{56,64},{64,... | collective-permute-start | bytes 786440 | tf_op jit(solution)/shard_map/ppermute | solution.py:381
  15.9 1.6 %collective-permute-start.2 = (f32[2,32,128]{2,1,0:T(8,128)S(1)}, f32[2,32,128]{2,1,0:T(8,128)S(1)}, u32[]{:S(2)}, u32[]{:S(2)}) collective-permute-start(f32[2,32,128]{2,1,0:T(8,128)S(1)} %get-tuple-element.31), channel_id=1, source_target_pairs={{0,7},{1,2},{2,1},{3,4},{4,3},{5,6},{6,5},{7,0},{8,15},{9,10},{10,... | collective-permute-start | bytes 98312 | tf_op jit(solution)/shard_map/ppermute | solution.py:381
  17.5 0.5 collective-permute-start.3
  18.0 3.9 %advect.1 = (f32[2048,128]{1,0:T(8,128)S(1)}, f32[2048,128]{1,0:T(8,128)S(1)}, f32[4096,128]{1,0:T(8,128)S(1)}, f32[64,128]{1,0:T(8,128)S(1)}, f32[32,128]{1,0:T...) custom-call(s32[1,1,8,64]{3,2,1,0:T(8,128)} %places.1, ...), custom_call_target="tpu_custom_call" | custom-call | bytes 18000000 | tf_op jit(solution)/shard_map/advect/pallas_call | solution.py:401
  21.9 7.7 %collective-permute-done.2.hyb = f32[2,32,128]{2,1,0:T(8,128)S(1)} collective-permute-done((f32[2,32,128]{2,1,0:T(8,128)S(1)}, f32[2,32,128]{2,1,0:T(8,128)S(1)}, u32[]{:S(2)}, u32[]{:S(2)}) %collective-permute-start.2) | collective-permute-done | bytes 32800 | tf_op jit(solution)/shard_map/ppermute | solution.py:381
  29.6 0.0 collective-permute-done.3.hya
  29.6 0.0 collective-permute-done.hxb.mb
  29.6 0.0 collective-permute-done.1.hxa.ma
  29.6 0.0 copy-start
  29.6 0.0 copy-start.1
  29.6 0.0 copy-start.2
  29.6 1.7 %fix_edges.1 = (f32[2048,128]{1,0:T(8,128)S(1)}, f32[2048,128]{1,0:T(8,128)S(1)}, f32[4096,128]{1,0:T(8,128)S(1)}, f32[3,64,128]{2,1,0:T(8,128)S(1)}, f32[3,64,128]{2,1,0:T(8,128)S(1)}) custom-call(s32[1,1,8,64]{3,2,1,0:T(8,128)} %places.1, s32[1,1,8]{2,1,0:T(1,128)} %tallies.1, ...), custom_call_target="tpu_custom_call", output_to_operand_aliasing={{0}: (13, {}), {1}: (14, {}), {2}: (15, {})} | custom-call | bytes 3000000 | tf_op jit(solution)/shard_map/fix_edges/pallas_call | solution.py:406
  31.3 0.1 collective-permute-start.4
  31.4 7.5 %collective-permute-start.5 = (f32[3,64,128]{2,1,0:T(8,128)S(1)}, f32[3,64,128]{2,1,0:T(8,128)S(1)}, u32[]{:S(2)}, u32[]{:S(2)}) collective-permute-start(f32[3,64,128]{2,1,0:T(8,128)S(1)} %get-tuple-element.50), channel_id=1, source_target_pairs={{0,248},{8,16},{16,8},{24,32},{32,24},{40,48},{48,40},{56,64},{64,... | collective-permute-start | bytes 294920 | tf_op jit(solution)/shard_map/ppermute | solution.py:381
  38.9 4.5 %grow.1 = (f32[3,2048,128]{2,1,0:T(8,128)}, f32[2048,128]{1,0:T(8,128)S(1)}, f32[2,3,64,128]{3,2,1,0:T(8,128)S(1)}) custom-call(s32[1,1,8,64]{3,2,1,0:T(8,128)S(1)} %copy-done.1, s32[1,1,8]{2,1,0:T(1,128)S(1)} %copy-done.2, s32[2048]{0:T(1024)S(1)} %copy-done, f32[4096,128]{1,0:T(8,128)S(1)} %get-tuple-element.40.table, ...), custom_call_target="tpu_custom_call" | custom-call | bytes 18000000 | tf_op jit(solution)/shard_map/grow/pallas_call | solution.py:414
  43.4 0.0 collective-permute-done.4.ra
  43.4 2.4 %collective-permute-done.5.rb = f32[3,64,128]{2,1,0:T(8,128)S(1)} collective-permute-done((f32[3,64,128]{2,1,0:T(8,128)S(1)}, f32[3,64,128]{2,1,0:T(8,128)S(1)}, u32[]{:S(2)}, u32[]{:S(2)}) %collective-permute-start.5) | collective-permute-done | bytes 98336 | tf_op jit(solution)/shard_map/ppermute | solution.py:381
  45.9 0.1 forward.1
  45.9 0.5 collective-permute-start.6
  46.4 6.1 %deposit.1 = (f32[2048,128]{1,0:T(8,128)}, f32[2048,128]{1,0:T(8,128)}) custom-call(s32[2048]{0:T(1024)S(1)} %copy-done, f32[2048,128]{1,0:T(8,128)S(1)} %get-tuple-element.43.cond, f32[2048,128]{1,0:T(8,128)S(1)} %get-tuple-element.44.aq, f32[2048,128]{1,0:T(8,128)S(1)} %get-tuple-element.45.at), custom_call_target="tpu_custom_call" | custom-call | bytes 18000000 | tf_op jit(solution)/shard_map/deposit/pallas_call | solution.py:422
  52.5 0.0 collective-permute-done.6.ya
  52.5 3.2 %collective-permute-done.7.yb = f32[3,3,64,128]{3,2,1,0:T(8,128)S(1)} collective-permute-done((f32[3,3,64,128]{3,2,1,0:T(8,128)S(1)}, f32[3,3,64,128]{3,2,1,0:T(8,128)S(1)}, u32[]{:S(2)}, u32[]{:S(2)}) %collective-permute-start.7) | collective-permute-done | bytes 294944 | tf_op jit(solution)/shard_map/ppermute | solution.py:381
  55.7 1.0 %arrive.1 = f32[8,3,64,128]{3,2,1,0:T(8,128)} custom-call(f32[3,64,128]{2,1,0:T(8,128)S(1)} %collective-permute-done.4.ra, f32[3,64,128]{2,1,0:T(8,128)S(1)} %collective-permute-done.5.rb, f32[8,64,128]{2,1,0:T(8,128)S(1)} %collective-permute-done.1.hxa.ma, f32[8,64,128]{2,1,0:T(8,128)S(1)} %collective-permute-done.hxb.mb, ...), custom_call_target="tpu_custom_call" | custom-call | bytes 3000000 | tf_op jit(solution)/shard_map/arrive/pallas_call | solution.py:427
  (5 shorter events, 0.0 us)
Async XLA Ops:
  3.5 26.1 %collective-permute-start = (f32[8,64,128]{2,1,0:T(8,128)S(1)}, f32[8,64,128]{2,1,0:T(8,128)S(1)}, u32[]{:S(2)}, u32[]{:S(2)}) collective-permute-start(f32[8,64,128]{2,1,0:T(8,128)S(1)} %get-tuple-element.29.xb), channel_id=1, source_target_pairs={{0,248},{8,16},{16,8},{24,32},{32,24},{40,48},{48,40},{56,64},{64,... | collective-permute-start | bytes 786440 | tf_op jit(solution)/shard_map/ppermute | solution.py:381
  15.9 13.6 %collective-permute-start.1 = (f32[8,64,128]{2,1,0:T(8,128)S(1)}, f32[8,64,128]{2,1,0:T(8,128)S(1)}, u32[]{:S(2)}, u32[]{:S(2)}) collective-permute-start(f32[8,64,128]{2,1,0:T(8,128)S(1)} %get-tuple-element.30.xa), channel_id=1, source_target_pairs={{0,8},{8,0},{16,24},{24,16},{32,40},{40,32},{48,56},{56,48},{64,72... | collective-permute-start | bytes 786440 | tf_op jit(solution)/shard_map/ppermute | solution.py:381
  15.9 13.6 %collective-permute-start.2 = (f32[2,32,128]{2,1,0:T(8,128)S(1)}, f32[2,32,128]{2,1,0:T(8,128)S(1)}, u32[]{:S(2)}, u32[]{:S(2)}) collective-permute-start(f32[2,32,128]{2,1,0:T(8,128)S(1)} %get-tuple-element.31), channel_id=1, source_target_pairs={{0,7},{1,2},{2,1},{3,4},{4,3},{5,6},{6,5},{7,0},{8,15},{9,10},{10,... | collective-permute-start | bytes 98312 | tf_op jit(solution)/shard_map/ppermute | solution.py:381
  17.5 12.0 %collective-permute-start.3 = (f32[2,32,128]{2,1,0:T(8,128)S(1)}, f32[2,32,128]{2,1,0:T(8,128)S(1)}, u32[]{:S(2)}, u32[]{:S(2)}) collective-permute-start(f32[2,32,128]{2,1,0:T(8,128)S(1)} %get-tuple-element.32), channel_id=1, source_target_pairs={{0,1},{1,0},{2,3},{3,2},{4,5},{5,4},{6,7},{7,6},{8,9},{9,8},{10,11... | collective-permute-start | bytes 98312 | tf_op jit(solution)/shard_map/ppermute | solution.py:381
  29.6 9.3 %copy-start = (s32[2048]{0:T(1024)S(1)}, s32[2048]{0:T(1024)}, u32[]{:S(2)}) copy-start(s32[2048]{0:T(1024)} %home.3) | copy-start | bytes 24580
  29.6 9.3 %copy-start.1 = (s32[1,1,8,64]{3,2,1,0:T(8,128)S(1)}, s32[1,1,8,64]{3,2,1,0:T(8,128)}, u32[]{:S(2)}) copy-start(s32[1,1,8,64]{3,2,1,0:T(8,128)} %places.1) | copy-start | bytes 6148
  29.6 9.3 %copy-start.2 = (s32[1,1,8]{2,1,0:T(1,128)S(1)}, s32[1,1,8]{2,1,0:T(1,128)}, u32[]{:S(2)}) copy-start(s32[1,1,8]{2,1,0:T(1,128)} %tallies.1) | copy-start | bytes 100
  31.3 12.2 %collective-permute-start.4 = (f32[3,64,128]{2,1,0:T(8,128)S(1)}, f32[3,64,128]{2,1,0:T(8,128)S(1)}, u32[]{:S(2)}, u32[]{:S(2)}) collective-permute-start(f32[3,64,128]{2,1,0:T(8,128)S(1)} %get-tuple-element.49), channel_id=1, source_target_pairs={{0,8},{8,0},{16,24},{24,16},{32,40},{40,32},{48,56},{56,48},{64,72... | collective-permute-start | bytes 294920 | tf_op jit(solution)/shard_map/ppermute | solution.py:381
  31.4 14.5 %collective-permute-start.5 = (f32[3,64,128]{2,1,0:T(8,128)S(1)}, f32[3,64,128]{2,1,0:T(8,128)S(1)}, u32[]{:S(2)}, u32[]{:S(2)}) collective-permute-start(f32[3,64,128]{2,1,0:T(8,128)S(1)} %get-tuple-element.50), channel_id=1, source_target_pairs={{0,248},{8,16},{16,8},{24,32},{32,24},{40,48},{48,40},{56,64},{64,... | collective-permute-start | bytes 294920 | tf_op jit(solution)/shard_map/ppermute | solution.py:381
  45.9 6.6 %collective-permute-start.6 = (f32[3,3,64,128]{3,2,1,0:T(8,128)S(1)}, f32[3,3,64,128]{3,2,1,0:T(8,128)S(1)}, u32[]{:S(2)}, u32[]{:S(2)}) collective-permute-start(f32[3,3,64,128]{3,2,1,0:T(8,128)S(1)} %get-tuple-element.52), channel_id=1, source_target_pairs={{0,1},{1,0},{2,3},{3,2},{4,5},{5,4},{6,7},{7,6},{8,9},{9,8},{10,11... | collective-permute-start | bytes 884744 | tf_op jit(solution)/shard_map/ppermute | solution.py:381
  46.4 9.3 %collective-permute-start.7 = (f32[3,3,64,128]{3,2,1,0:T(8,128)S(1)}, f32[3,3,64,128]{3,2,1,0:T(8,128)S(1)}, u32[]{:S(2)}, u32[]{:S(2)}) collective-permute-start(f32[3,3,64,128]{3,2,1,0:T(8,128)S(1)} %get-tuple-element.53), channel_id=1, source_target_pairs={{0,7},{1,2},{2,1},{3,4},{4,3},{5,6},{6,5},{7,0},{8,15},{9,10},{10,... | collective-permute-start | bytes 884744 | tf_op jit(solution)/shard_map/ppermute | solution.py:381

commit v2 on v1

--- a/solution.py
+++ b/solution.py
@@ -15,6 +15,7 @@
 CROWS = ROWS // CHUNKS
 LANES_ACC = 4
 UNROLL = 8
+FIRST = 1024
 POWER = 17.27 * (273.15 - 35.86) * math.log2(math.e)
 SHIFT = 17.27 * math.log2(math.e) + math.log2(3.8)
 F32 = jnp.float32
@@ -168,12 +169,13 @@
 
 
 def kernel_advect(
-    places_h, q_h, t_h, we_h, wn_h, parts_h,
-    aq, at, table, cw, cs, radius, leave_b, leave_a,
-    qv, tv, wev, wnv, places, sems, psem,
+    places_h, tallies_h, rest, q_h, t_h, we_h, wn_h, parts_h,
+    aq, at, table, cw, cs, radius, leave_b, leave_a, along_y,
+    qv, tv, wev, wnv, places, tallies, sems, psem,
 ):
     copies = [
         pltpu.make_async_copy(places_h, places, psem.at[0]),
+        pltpu.make_async_copy(tallies_h, tallies, psem.at[2]),
         pltpu.make_async_copy(parts_h.at[0], radius, psem.at[1]),
     ]
     for c in copies:
@@ -185,11 +187,48 @@
         c.wait()
     for leave, n, d in gx_sends((leave_b, leave_a)):
         fetch_rows(SLOTS, lambda s, d=d: places[0, 0, d, s], [(radius, leave.at[n])])
+    slot = lax.broadcasted_iota(jnp.int32, (SLOTS, LEV), 0)
+    for n, d in enumerate((2, 3)):
+        for p in range(2):
+            dst = along_y.at[n, p]
+            fetch_rows(SLOTS, lambda s, d=d: places[0, 0, d, s], [(rest.at[p], dst)])
+            dst[...] = jnp.where(slot < tallies[0, 0, d], dst[...], 0.0)
+
+
+def steer(sends, place, north, south, of_b, of_a):
+    ox, oy = odd_x(), odd_y()
+    for n in range(3):
+        if n == 0:
+            up, down = north, south
+        else:
+            one, two = (of_a, of_b) if n == 1 else (of_b, of_a)
+            up = jnp.where(ox, one(1), two(1))
+            down = jnp.where(ox, one(2), two(2))
+        sends[0][place(n)] = jnp.where(oy, up, down)
+        sends[1][place(n)] = jnp.where(oy, down, up)
+
+
+def scatter_rows(home, cond, acc, start, stop):
+    half = lax.broadcasted_iota(jnp.int32, (1, LEV), 1) // 64
+
+    def scatter(g, _):
+        b0 = g * LANES_ACC
+        where = [home[b0 + k] for k in range(LANES_ACC)]
+        rows = [pl.ds(c >> 1, 1) for c in where]
+        sums = [
+            acc[k, rows[k]] + jnp.where(half == (where[k] & 1), cond[pl.ds(b0 + k, 1)], 0.0)
+            for k in range(LANES_ACC)
+        ]
+        for k in range(LANES_ACC):
+            acc[k, rows[k]] = sums[k]
+        return 0
+
+    lax.fori_loop(start // LANES_ACC, stop // LANES_ACC, scatter, 0, unroll=UNROLL)
 
 
 def kernel_fix(
-    places_h, tallies_h, home_h, hxb, hxa, hyb, hya, cw, cs, leave_b, leave_a, xb, xa, aq_in, at_in, table_in,
-    aq, at, table, send_b, send_a, got, places, tallies, home, sems,
+    places_h, tallies_h, home_h, hxb, hxa, hyb, hya, cw, cs, leave_b, leave_a, xb, xa, along_y, aq_in, at_in, table_in,
+    aq, at, table, send_b, send_a, rest_b, rest_a, got, places, tallies, home, sems,
 ):
     lists = ((places_h, places), (tallies_h, tallies), (home_h, home))
     copies = [pltpu.make_async_copy(a, b, sems.at[k]) for k, (a, b) in enumerate(lists)]
@@ -219,9 +258,14 @@
         fetch_rows(SLOTS, lambda s, d=d: home[places[0, 0, d, s]], [(table, got)])
         square = growth_base(radii[k // 3][n], rests[k // 3][3 + 2 * n]) + 20.0 * got[...]
         send[n] = jnp.where(slot < tallies[0, 0, d], root(jnp.maximum(square, 0.25)), 0.0)
-
-
-def kernel_grow(places, tallies, home, table, radius, rest, parts_out, cond, ahead, got, new_r, sems, psem):
+    for p in range(2):
+        steer(
+            (rest_b, rest_a), lambda n, p=p: 2 * n + p, along_y[0, p], along_y[1, p],
+            lambda n, p=p: hxb[2 + 2 * n + p], lambda n, p=p: hxa[2 + 2 * n + p],
+        )
+
+
+def kernel_grow(places, tallies, home, table, radius, rest, parts_out, cond, ahead, acc, got, new_r, sems, psem):
     copies = [pltpu.make_async_copy(rest.at[p], parts_out.at[1 + p], psem.at[p]) for p in range(2)]
     for c in copies:
         c.start()
@@ -250,59 +294,27 @@
         outs.append(c)
     slot = lax.broadcasted_iota(jnp.int32, (SLOTS, LEV), 0)
     for n, d in enumerate((2, 3)):
-        fetch_rows(
-            SLOTS,
-            lambda s, d=d: places[0, 0, d, s],
-            [(new_r, ahead.at[n, 0]), (rest.at[0], ahead.at[n, 1]), (rest.at[1], ahead.at[n, 2])],
-        )
-        live = slot < tallies[0, 0, d]
-        for p in range(3):
-            ahead[n, p] = jnp.where(live, ahead[n, p], 0.0)
-    for c in outs + copies:
-        c.wait()
-
-
-def piece(radius, rest, n, p):
-    return radius[n] if p == 0 else rest[1 + 2 * n + p]
-
-
-def kernel_forward(ahead, ra, rb, ma, mb, ya, yb):
-    ox, oy = odd_x(), odd_y()
-    a, b = (ra, ma), (rb, mb)
-    for n in range(3):
-        for p in range(3):
-            if n == 0:
-                up, down = ahead[0, p], ahead[1, p]
-            else:
-                one, two = (a, b) if n == 1 else (b, a)
-                up = jnp.where(ox, piece(*one, 1, p), piece(*two, 1, p))
-                down = jnp.where(ox, piece(*one, 2, p), piece(*two, 2, p))
-            ya[n, p] = jnp.where(oy, down, up)
-            yb[n, p] = jnp.where(oy, up, down)
-
-
-def kernel_deposit(home, cond, aq, at, q_out, t_out, acc, qo, to, sems):
+        dst = ahead.at[n]
+        fetch_rows(SLOTS, lambda s, d=d: places[0, 0, d, s], [(new_r, dst)])
+        dst[...] = jnp.where(slot < tallies[0, 0, d], dst[...], 0.0)
+
     def clear(g, _):
         for k in range(LANES_ACC):
             acc[k, pl.ds(pl.multiple_of(g * 128, 128), 128)] = jnp.zeros((128, LEV), F32)
         return 0
 
     lax.fori_loop(0, ROWS // 128, clear, 0)
-    half = lax.broadcasted_iota(jnp.int32, (1, LEV), 1) // 64
-
-    def scatter(g, _):
-        b0 = g * LANES_ACC
-        where = [home[b0 + k] for k in range(LANES_ACC)]
-        rows = [pl.ds(c >> 1, 1) for c in where]
-        sums = [
-            acc[k, rows[k]] + jnp.where(half == (where[k] & 1), cond[pl.ds(b0 + k, 1)], 0.0)
-            for k in range(LANES_ACC)
-        ]
-        for k in range(LANES_ACC):
-            acc[k, rows[k]] = sums[k]
-        return 0
-
-    lax.fori_loop(0, NB // LANES_ACC, scatter, 0, unroll=UNROLL)
+    scatter_rows(home, cond, acc, 0, FIRST)
+    for c in outs + copies:
+        c.wait()
+
+
+def kernel_forward(ahead, rb, ra, yb, ya):
+    steer((yb, ya), lambda n: n, ahead[0], ahead[1], lambda n: rb[n], lambda n: ra[n])
+
+
+def kernel_deposit(home, cond, aq, at, acc_in, q_out, t_out, acc, qo, to, sems):
+    scatter_rows(home, cond, acc, FIRST, NB)
     outs = []
     for j in range(CHUNKS):
 
@@ -325,22 +337,20 @@
         c.wait()
 
 
-def kernel_arrive(ra, rb, ma, mb, ya, yb, out, buf, sems):
+def kernel_arrive(rb, ra, mb, ma, yrb, yra, ymb, yma, out, buf, sems):
     ox, oy = odd_x(), odd_y()
     copies = []
-
-    def ship(d):
+    for d, odd, one, two, n, skip in (
+        (0, ox, (ra, ma), (rb, mb), 0, 2), (1, ox, (rb, mb), (ra, ma), 0, 2),
+        *((NORTH[n], oy, (yra, yma), (yrb, ymb), n, 0) for n in range(3)),
+        *((SOUTH[n], oy, (yrb, ymb), (yra, yma), n, 0) for n in range(3)),
+    ):
+        buf[d, 0] = jnp.where(odd, one[0][n], two[0][n])
+        for p in range(2):
+            k = skip + 2 * n + p
+            buf[d, 1 + p] = jnp.where(odd, one[1][k], two[1][k])
         copies.append(pltpu.make_async_copy(buf.at[d], out.at[d], sems.at[d]))
         copies[-1].start()
-
-    for d, one, two in ((0, (ra, ma), (rb, mb)), (1, (rb, mb), (ra, ma))):
-        for p in range(3):
-            buf[d, p] = jnp.where(ox, piece(*one, 0, p), piece(*two, 0, p))
-        ship(d)
-    for n in range(3):
-        for d, one, two in ((NORTH[n], ya, yb), (SOUTH[n], yb, ya)):
-            buf[d] = jnp.where(oy, one[n], two[n])
-            ship(d)
     for c in copies:
         c.wait()
 
@@ -388,7 +398,8 @@
     places_h, tallies_h, home_h = in_hbm(places), in_hbm(tallies), in_hbm(home)
     places_s, tallies_s = pltpu.SMEM((1, 1, 8, SLOTS), jnp.int32), pltpu.SMEM((1, 1, 8), jnp.int32)
     cells, table_of, blocks = vmem(ROWS, LEV), vmem(2 * ROWS, LEV), vmem(NB, LEV)
-    pay, radii = vmem(3, 3, SLOTS, LEV), vmem(3, SLOTS, LEV)
+    pairs, radii = vmem(6, SLOTS, LEV), vmem(3, SLOTS, LEV)
+    sums = vmem(LANES_ACC, ROWS, LEV)
     xb, xa, yb, ya, rest = call(
         kernel_send, "send_edges", 1, [ANY] * 5, [VM] * 5,
         [vmem(8, CY, LEV)] * 2 + [vmem(2, CX, LEV)] * 2 + [vmem(2, NB, LEV)],
@@ -398,36 +409,38 @@
     hxa = swapped(xa, "gx", 0)
     hyb = swapped(yb, "gy", 1)
     hya = swapped(ya, "gy", 0)
-    aq, at, table, cw, cs, radius, leave_b, leave_a = call(
-        kernel_advect, "advect", 6, [ANY] * 6, [VM] * 8,
-        [cells, cells, table_of, vmem(CY, LEV), vmem(CX, LEV), blocks, radii, radii],
-        [cells] * 4 + [places_s, dma(4, CHUNKS), dma(2)],
-    )(places_h, *flat, parts)
-    aq, at, table, rb, ra = call(
-        kernel_fix, "fix_edges", 1, [ANY] * 3 + [VM] * 13, [VM] * 5,
-        [cells, cells, table_of, radii, radii],
+    aq, at, table, cw, cs, radius, leave_b, leave_a, along_y = call(
+        kernel_advect, "advect", 6, [ANY] * 2 + [VM] + [ANY] * 5, [VM] * 9,
+        [cells, cells, table_of, vmem(CY, LEV), vmem(CX, LEV), blocks, radii, radii,
+         vmem(2, 2, SLOTS, LEV)],
+        [cells] * 4 + [places_s, tallies_s, dma(4, CHUNKS), dma(3)],
+    )(places_h, tallies_h, rest, *flat, parts)
+    aq, at, table, rb, ra, ymb, yma = call(
+        kernel_fix, "fix_edges", 1, [ANY] * 3 + [VM] * 14, [VM] * 7,
+        [cells, cells, table_of, radii, radii, pairs, pairs],
         [vmem(SLOTS, LEV), places_s, tallies_s, pltpu.SMEM((NB,), jnp.int32), dma(3)],
-        {13: 0, 14: 1, 15: 2},
-    )(places_h, tallies_h, home_h, hxb, hxa, hyb, hya, cw, cs, leave_b, leave_a, xb, xa, aq, at, table)
+        {14: 0, 15: 1, 16: 2},
+    )(places_h, tallies_h, home_h, hxb, hxa, hyb, hya, cw, cs, leave_b, leave_a, xb, xa, along_y, aq, at, table)
     rb = swapped(rb, "gx", 1)
     ra = swapped(ra, "gx", 0)
-    parts_out, cond, ahead = call(
-        kernel_grow, "grow", 6, [SM] * 3 + [VM] * 3, [ANY, VM, VM],
-        [hbm(3, NB, LEV), blocks, vmem(2, 3, SLOTS, LEV)],
+    ymb = swapped(ymb, "gy", 1)
+    yma = swapped(yma, "gy", 0)
+    parts_out, cond, ahead, acc = call(
+        kernel_grow, "grow", 6, [SM] * 3 + [VM] * 3, [ANY, VM, VM, VM],
+        [hbm(3, NB, LEV), blocks, vmem(2, SLOTS, LEV), sums],
         [vmem(2, NB // CHUNKS, LEV), blocks, dma(CHUNKS), dma(2)],
     )(places, tallies, home, table, radius, rest)
-    ya, yb = call(kernel_forward, "forward", 1, [VM] * 5, [VM] * 2, [pay, pay], [])(ahead, ra, rb, hxa, hxb)
-    gyb = swapped(yb, "gy", 1)
-    gya = swapped(ya, "gy", 0)
-    q_out, t_out = call(
-        kernel_deposit, "deposit", 6, [SM] + [VM] * 3, [ANY, ANY],
-        [hbm(ROWS, LEV), hbm(ROWS, LEV)],
-        [vmem(LANES_ACC, ROWS, LEV), cells, cells, dma(2, CHUNKS)],
-    )(home, cond, aq, at)
+    yb, ya = call(kernel_forward, "forward", 1, [VM] * 3, [VM] * 2, [radii, radii], [])(ahead, rb, ra)
+    yrb = swapped(yb, "gy", 1)
+    yra = swapped(ya, "gy", 0)
+    q_out, t_out, _ = call(
+        kernel_deposit, "deposit", 4, [SM] + [VM] * 4, [ANY, ANY, VM],
+        [hbm(ROWS, LEV), hbm(ROWS, LEV), sums], [cells, cells, dma(2, CHUNKS)], {4: 2},
+    )(home, cond, aq, at, acc)
     arrived = call(
-        kernel_arrive, "arrive", 1, [VM] * 6, ANY, hbm(8, 3, SLOTS, LEV),
+        kernel_arrive, "arrive", 1, [VM] * 8, ANY, hbm(8, 3, SLOTS, LEV),
         [vmem(8, 3, SLOTS, LEV), dma(8)],
-    )(ra, rb, hxa, hxb, gya, gyb)
+    )(rb, ra, hxb, hxa, yrb, yra, ymb, yma)
     incoming = arrived.transpose(0, 2, 1, 3)[None, None]
     shape = (CX, CY, LEV)
     return q_out.reshape(shape), t_out.reshape(shape), parts_out.transpose(1, 0, 2), incoming

time: 56.9 us -> 55.5 us (0.975)
  waiting for transfers between devices: 13.3 us -> 7.2 us
  starting transfers between devices: 22.6 us -> 27.6 us
    ppermute x8 -> x10, waiting for transfers between devices: 13.3 us -> 7.2 us  [swapped(): lax.ppermute(value, axis, [(i, (i + step[i]) % count) for i in range(coun...]
    ppermute x8 -> x10, starting transfers between devices: 22.6 us -> 27.6 us  [swapped(): lax.ppermute(value, axis, [(i, (i + step[i]) % count) for i in range(coun...]
  transfers between devices with their start and end apart: 8 -> 10, of which waited for: 3 -> 1; matrix products, arithmetic and copies ran while one was open for 0% -> 0% of each run, Pallas kernels for 26% -> 26%
where the time goes in v2:
time: 55.5 us; the launch traced here: 55.4 us
  starting transfers between devices  27.6 us (50%)
  Pallas kernels  19.8 us (36%)
  waiting for transfers between devices  7.2 us (13%)
  between operations  0.77 us (1%)
    ppermute x10, starting transfers between devices, swapped(): lax.ppermute(value, axis, [(i, (i + step[i]) % count) for i in range(coun...  27.6 us
    ppermute x10, waiting for transfers between devices, swapped(): lax.ppermute(value, axis, [(i, (i + step[i]) % count) for i in range(coun...  7.2 us
    pallas_call x1, Pallas kernels, body(): call(kernel_grow, 'grow', 6, [SM] * 3 + [VM] * 3, [ANY, VM, VM, VM], [hbm...  5.91 us
    pallas_call x1, Pallas kernels, body(): call(kernel_advect, 'advect', 6, [ANY] * 2 + [VM] + [ANY] * 5, [VM] * 9,...  4.36 us
    pallas_call x1, Pallas kernels, body(): call(kernel_deposit, 'deposit', 4, [SM] + [VM] * 4, [ANY, ANY, VM], [hbm(...  4.04 us
    pallas_call x1, Pallas kernels, body(): call(kernel_send, 'send_edges', 1, [ANY] * 5, [VM] * 5, [vmem(8, CY, LEV)...  2.82 us
    pallas_call x1, Pallas kernels, body(): call(kernel_fix, 'fix_edges', 1, [ANY] * 3 + [VM] * 14, [VM] * 7, [cells,...  1.68 us
  transfers between devices with their start and end apart: 10, of which 1 were waited for; matrix products, arithmetic and copies ran while one was open for 0% of the time, Pallas kernels for 26%

profile of v2, /device:TPU:1, one launch (start us, length us, event | category | flops | bytes accessed | tf_op | source)
XLA Modules:
  0.0 55.4 jit_solution(11494789997465053035)
XLA Ops:
  0.6 2.8 %send_edges.1 = (f32[8,64,128]{2,1,0:T(8,128)S(1)}, f32[8,64,128]{2,1,0:T(8,128)S(1)}, f32[2,32,128]{2,1,0:T(8,128)S(1)}, f32[2,32,128]{2,1,0:T(8,128)S(1)}, f32[2,2048,128]{2,1,0:T(8,128)S(1)}) custom-call(f32[32,64,128]{2,1,0:T(8,128)} %q_h.1, f32[32,64,128]{2,1,0:T(8,128)} %t_h.1, s32[1,1,8,64]{3,2,1,0:T(8,128)} %places.1, s32[1,1,8]{2,1,0:T(1,128)} %tallies.1, ...), custom_call_target="tpu_custom_call" | custom-call | bytes 3000000 | tf_op jit(solution)/shard_map/send_edges/pallas_call | solution.py:403
  3.5 12.5 %collective-permute-start = (f32[8,64,128]{2,1,0:T(8,128)S(1)}, f32[8,64,128]{2,1,0:T(8,128)S(1)}, u32[]{:S(2)}, u32[]{:S(2)}) collective-permute-start(f32[8,64,128]{2,1,0:T(8,128)S(1)} %get-tuple-element.33.xb), channel_id=1, source_target_pairs={{0,248},{8,16},{16,8},{24,32},{32,24},{40,48},{48,40},{56,64},{64,... | collective-permute-start | bytes 786440 | tf_op jit(solution)/shard_map/ppermute | solution.py:391
  15.9 1.6 %collective-permute-start.2 = (f32[2,32,128]{2,1,0:T(8,128)S(1)}, f32[2,32,128]{2,1,0:T(8,128)S(1)}, u32[]{:S(2)}, u32[]{:S(2)}) collective-permute-start(f32[2,32,128]{2,1,0:T(8,128)S(1)} %get-tuple-element.35), channel_id=1, source_target_pairs={{0,7},{1,2},{2,1},{3,4},{4,3},{5,6},{6,5},{7,0},{8,15},{9,10},{10,... | collective-permute-start | bytes 98312 | tf_op jit(solution)/shard_map/ppermute | solution.py:391
  17.5 0.5 collective-permute-start.3
  18.0 4.4 %advect.1 = (f32[2048,128]{1,0:T(8,128)S(1)}, f32[2048,128]{1,0:T(8,128)S(1)}, f32[4096,128]{1,0:T(8,128)S(1)}, f32[64,128]{1,0:T(8,128)S(1)}, f32[32,128]{1,0:T...) custom-call(s32[1,1,8,64]{3,2,1,0:T(8,128)} %places.1, ...), custom_call_target="tpu_custom_call" | custom-call | bytes 18000000 | tf_op jit(solution)/shard_map/advect/pallas_call | solution.py:412
  22.3 0.0 copy-start
  22.4 0.0 copy-start.1
  22.4 0.0 copy-start.2
  22.4 7.2 %collective-permute-done.2.hyb = f32[2,32,128]{2,1,0:T(8,128)S(1)} collective-permute-done((f32[2,32,128]{2,1,0:T(8,128)S(1)}, f32[2,32,128]{2,1,0:T(8,128)S(1)}, u32[]{:S(2)}, u32[]{:S(2)}) %collective-permute-start.2) | collective-permute-done | bytes 32800 | tf_op jit(solution)/shard_map/ppermute | solution.py:391
  29.6 0.0 collective-permute-done.hxb.mb
  29.6 0.0 collective-permute-done.1.hxa.ma
  29.6 1.7 %fix_edges.1 = (f32[2048,128]{1,0:T(8,128)S(1)}, f32[2048,128]{1,0:T(8,128)S(1)}, f32[4096,128]{1,0:T(8,128)S(1)}, f32[3,64,128]{2,1,0:T(8,128)S(1)}, f32[3,64,1...) custom-call(s32[1,1,8,64]{3,2,1,0:T(8,128)} %places.1, ...), custom_call_target="tpu_custom_call", output_to_operand_aliasing={{0}: (14, {}), {1}: (15, {}), {2}: (16, {})} | custom-call | bytes 3000000 | tf_op jit(solution)/shard_map/fix_edges/pallas_call | solution.py:418
  31.3 7.5 %collective-permute-start.4 = (f32[3,64,128]{2,1,0:T(8,128)S(1)}, f32[3,64,128]{2,1,0:T(8,128)S(1)}, u32[]{:S(2)}, u32[]{:S(2)}) collective-permute-start(f32[3,64,128]{2,1,0:T(8,128)S(1)} %get-tuple-element.55), channel_id=1, source_target_pairs={{0,248},{8,16},{16,8},{24,32},{32,24},{40,48},{48,40},{56,64},{64,... | collective-permute-start | bytes 294920 | tf_op jit(solution)/shard_map/ppermute | solution.py:391
  38.7 0.0 collective-permute-start.5
  38.8 2.7 %collective-permute-start.8 = (f32[6,64,128]{2,1,0:T(8,128)S(1)}, f32[6,64,128]{2,1,0:T(8,128)S(1)}, u32[]{:S(2)}, u32[]{:S(2)}) collective-permute-start(f32[6,64,128]{2,1,0:T(8,128)S(1)} %get-tuple-element.60), channel_id=1, source_target_pairs={{0,7},{1,2},{2,1},{3,4},{4,3},{5,6},{6,5},{7,0},{8,15},{9,10},{10,... | collective-permute-start | bytes 589832 | tf_op jit(solution)/shard_map/ppermute | solution.py:391
  41.4 5.9 %grow.1 = (f32[3,2048,128]{2,1,0:T(8,128)}, f32[2048,128]{1,0:T(8,128)S(1)}, f32[2,64,128]{2,1,0:T(8,128)S(1)}, f32[4,2048,128]{2,1,0:T(8,128)S(1)}) custom-call(s32[1,1,8,64]{3,2,1,0:T(8,128)S(1)} %copy-done.1, s32[1,1,8]{2,1,0:T(1,128)S(1)} %copy-done.2, s32[2048]{0:T(1024)S(1)} %copy-done, f32[4096,128]{1,0:T(8,128)S(1)} %get-tuple-element.46.table, ...), custom_call_target="tpu_custom_call" | custom-call | bytes 18000000 | tf_op jit(solution)/shard_map/grow/pallas_call | solution.py:428
  47.4 0.0 collective-permute-done.4.rb
  47.4 0.1 collective-permute-start.6
  47.5 2.8 %collective-permute-start.7 = (f32[3,64,128]{2,1,0:T(8,128)S(1)}, f32[3,64,128]{2,1,0:T(8,128)S(1)}, u32[]{:S(2)}, u32[]{:S(2)}) collective-permute-start(f32[3,64,128]{2,1,0:T(8,128)S(1)} %get-tuple-element.59), channel_id=1, source_target_pairs={{0,1},{1,0},{2,3},{3,2},{4,5},{5,4},{6,7},{7,6},{8,9},{9,8},{10,11... | collective-permute-start | bytes 294920 | tf_op jit(solution)/shard_map/ppermute | solution.py:391
  50.3 4.0 %deposit.1 = (f32[2048,128]{1,0:T(8,128)}, f32[2048,128]{1,0:T(8,128)}, f32[4,2048,128]{2,1,0:T(8,128)S(1)}) custom-call(s32[2048]{0:T(1024)S(1)} %copy-done, f32[2048,128]{1,0:T(8,128)S(1)} %get-tuple-element.48.cond, f32[2048,128]{1,0:T(8,128)S(1)} %get-tuple-element.49.aq, f32[2048,128]{1,0:T(8,128)S(1)} %get-tuple-element.50.at, ...), custom_call_target="tpu_custom_call", output_to_operand_aliasing={{2}: (4, {})} | custom-call | bytes 12000000 | tf_op jit(solution)/shard_map/deposit/pallas_call | solution.py:436
  54.4 0.0 collective-permute-done.6.yrb
  54.4 0.0 collective-permute-done.8.ymb
  54.4 0.0 collective-permute-done.9.yma
  54.4 1.0 %arrive.1 = f32[8,3,64,128]{3,2,1,0:T(8,128)} custom-call(f32[3,64,128]{2,1,0:T(8,128)S(1)} %collective-permute-done.4.rb, f32[3,64,128]{2,1,0:T(8,128)S(1)} %collective-permute-done.5.ra, f32[8,64,128]{2,1,0:T(8,128)S(1)} %collective-permute-done.hxb.mb, f32[8,64,128]{2,1,0:T(8,128)S(1)} %collective-permute-done.1.hxa.ma, ...), custom_call_target="tpu_custom_call" | custom-call | bytes 3000000 | tf_op jit(solution)/shard_map/arrive/pallas_call | solution.py:440
  (9 shorter events, 0.0 us)
Async XLA Ops:
  3.5 26.1 %collective-permute-start = (f32[8,64,128]{2,1,0:T(8,128)S(1)}, f32[8,64,128]{2,1,0:T(8,128)S(1)}, u32[]{:S(2)}, u32[]{:S(2)}) collective-permute-start(f32[8,64,128]{2,1,0:T(8,128)S(1)} %get-tuple-element.33.xb), channel_id=1, source_target_pairs={{0,248},{8,16},{16,8},{24,32},{32,24},{40,48},{48,40},{56,64},{64,... | collective-permute-start | bytes 786440 | tf_op jit(solution)/shard_map/ppermute | solution.py:391
  15.9 13.6 %collective-permute-start.1 = (f32[8,64,128]{2,1,0:T(8,128)S(1)}, f32[8,64,128]{2,1,0:T(8,128)S(1)}, u32[]{:S(2)}, u32[]{:S(2)}) collective-permute-start(f32[8,64,128]{2,1,0:T(8,128)S(1)} %get-tuple-element.34.xa), channel_id=1, source_target_pairs={{0,8},{8,0},{16,24},{24,16},{32,40},{40,32},{48,56},{56,48},{64,72... | collective-permute-start | bytes 786440 | tf_op jit(solution)/shard_map/ppermute | solution.py:391
  15.9 13.6 %collective-permute-start.2 = (f32[2,32,128]{2,1,0:T(8,128)S(1)}, f32[2,32,128]{2,1,0:T(8,128)S(1)}, u32[]{:S(2)}, u32[]{:S(2)}) collective-permute-start(f32[2,32,128]{2,1,0:T(8,128)S(1)} %get-tuple-element.35), channel_id=1, source_target_pairs={{0,7},{1,2},{2,1},{3,4},{4,3},{5,6},{6,5},{7,0},{8,15},{9,10},{10,... | collective-permute-start | bytes 98312 | tf_op jit(solution)/shard_map/ppermute | solution.py:391
  17.5 12.0 %collective-permute-start.3 = (f32[2,32,128]{2,1,0:T(8,128)S(1)}, f32[2,32,128]{2,1,0:T(8,128)S(1)}, u32[]{:S(2)}, u32[]{:S(2)}) collective-permute-start(f32[2,32,128]{2,1,0:T(8,128)S(1)} %get-tuple-element.36), channel_id=1, source_target_pairs={{0,1},{1,0},{2,3},{3,2},{4,5},{5,4},{6,7},{7,6},{8,9},{9,8},{10,11... | collective-permute-start | bytes 98312 | tf_op jit(solution)/shard_map/ppermute | solution.py:391
  22.3 19.1 %copy-start = (s32[2048]{0:T(1024)S(1)}, s32[2048]{0:T(1024)}, u32[]{:S(2)}) copy-start(s32[2048]{0:T(1024)} %home.3) | copy-start | bytes 24580
  22.4 19.1 %copy-start.1 = (s32[1,1,8,64]{3,2,1,0:T(8,128)S(1)}, s32[1,1,8,64]{3,2,1,0:T(8,128)}, u32[]{:S(2)}) copy-start(s32[1,1,8,64]{3,2,1,0:T(8,128)} %places.1) | copy-start | bytes 6148
  22.4 19.1 %copy-start.2 = (s32[1,1,8]{2,1,0:T(1,128)S(1)}, s32[1,1,8]{2,1,0:T(1,128)}, u32[]{:S(2)}) copy-start(s32[1,1,8]{2,1,0:T(1,128)} %tallies.1) | copy-start | bytes 100
  31.3 16.1 %collective-permute-start.4 = (f32[3,64,128]{2,1,0:T(8,128)S(1)}, f32[3,64,128]{2,1,0:T(8,128)S(1)}, u32[]{:S(2)}, u32[]{:S(2)}) collective-permute-start(f32[3,64,128]{2,1,0:T(8,128)S(1)} %get-tuple-element.55), channel_id=1, source_target_pairs={{0,248},{8,16},{16,8},{24,32},{32,24},{40,48},{48,40},{56,64},{64,... | collective-permute-start | bytes 294920 | tf_op jit(solution)/shard_map/ppermute | solution.py:391
  38.7 8.6 %collective-permute-start.5 = (f32[3,64,128]{2,1,0:T(8,128)S(1)}, f32[3,64,128]{2,1,0:T(8,128)S(1)}, u32[]{:S(2)}, u32[]{:S(2)}) collective-permute-start(f32[3,64,128]{2,1,0:T(8,128)S(1)} %get-tuple-element.56), channel_id=1, source_target_pairs={{0,8},{8,0},{16,24},{24,16},{32,40},{40,32},{48,56},{56,48},{64,72... | collective-permute-start | bytes 294920 | tf_op jit(solution)/shard_map/ppermute | solution.py:391
  38.8 15.7 %collective-permute-start.8 = (f32[6,64,128]{2,1,0:T(8,128)S(1)}, f32[6,64,128]{2,1,0:T(8,128)S(1)}, u32[]{:S(2)}, u32[]{:S(2)}) collective-permute-start(f32[6,64,128]{2,1,0:T(8,128)S(1)} %get-tuple-element.60), channel_id=1, source_target_pairs={{0,7},{1,2},{2,1},{3,4},{4,3},{5,6},{6,5},{7,0},{8,15},{9,10},{10,... | collective-permute-start | bytes 589832 | tf_op jit(solution)/shard_map/ppermute | solution.py:391
  41.4 13.0 %collective-permute-start.9 = (f32[6,64,128]{2,1,0:T(8,128)S(1)}, f32[6,64,128]{2,1,0:T(8,128)S(1)}, u32[]{:S(2)}, u32[]{:S(2)}) collective-permute-start(f32[6,64,128]{2,1,0:T(8,128)S(1)} %get-tuple-element.61), channel_id=1, source_target_pairs={{0,1},{1,0},{2,3},{3,2},{4,5},{5,4},{6,7},{7,6},{8,9},{9,8},{10,11... | collective-permute-start | bytes 589832 | tf_op jit(solution)/shard_map/ppermute | solution.py:391
  47.4 7.0 %collective-permute-start.6 = (f32[3,64,128]{2,1,0:T(8,128)S(1)}, f32[3,64,128]{2,1,0:T(8,128)S(1)}, u32[]{:S(2)}, u32[]{:S(2)}) collective-permute-start(f32[3,64,128]{2,1,0:T(8,128)S(1)} %get-tuple-element.58), channel_id=1, source_target_pairs={{0,7},{1,2},{2,1},{3,4},{4,3},{5,6},{6,5},{7,0},{8,15},{9,10},{10,... | collective-permute-start | bytes 294920 | tf_op jit(solution)/shard_map/ppermute | solution.py:391
  47.5 6.9 %collective-permute-start.7 = (f32[3,64,128]{2,1,0:T(8,128)S(1)}, f32[3,64,128]{2,1,0:T(8,128)S(1)}, u32[]{:S(2)}, u32[]{:S(2)}) collective-permute-start(f32[3,64,128]{2,1,0:T(8,128)S(1)} %get-tuple-element.59), channel_id=1, source_target_pairs={{0,1},{1,0},{2,3},{3,2},{4,5},{5,4},{6,7},{7,6},{8,9},{9,8},{10,11... | collective-permute-start | bytes 294920 | tf_op jit(solution)/shard_map/ppermute | solution.py:391

commit v3 on v2

--- a/solution.py
+++ b/solution.py
@@ -15,7 +15,7 @@
 CROWS = ROWS // CHUNKS
 LANES_ACC = 4
 UNROLL = 8
-FIRST = 1024
+FIRST = 1536
 POWER = 17.27 * (273.15 - 35.86) * math.log2(math.e)
 SHIFT = 17.27 * math.log2(math.e) + math.log2(3.8)
 F32 = jnp.float32
@@ -104,7 +104,9 @@
     for p in range(2):
         planes[p].wait()
         for send, n, d in gx_sends((xb, xa)):
-            dst = send.at[2 + 2 * n + p]
+            if n == 0:
+                continue
+            dst = send.at[2 * n + p]
             fetch_rows(SLOTS, lambda s, d=d: places[0, 0, d, s], [(rest.at[p], dst)])
             dst[...] = jnp.where(slot < tallies[0, 0, d], dst[...], 0.0)
 
@@ -170,7 +172,7 @@
 
 def kernel_advect(
     places_h, tallies_h, rest, q_h, t_h, we_h, wn_h, parts_h,
-    aq, at, table, cw, cs, radius, leave_b, leave_a, along_y,
+    aq, at, table, cw, cs, radius, leave_b, leave_a, straight_b, straight_a, along_y,
     qv, tv, wev, wnv, places, tallies, sems, psem,
 ):
     copies = [
@@ -188,9 +190,14 @@
     for leave, n, d in gx_sends((leave_b, leave_a)):
         fetch_rows(SLOTS, lambda s, d=d: places[0, 0, d, s], [(radius, leave.at[n])])
     slot = lax.broadcasted_iota(jnp.int32, (SLOTS, LEV), 0)
-    for n, d in enumerate((2, 3)):
+    ox = odd_x()
+    straight = (
+        (straight_b, jnp.where(ox, EAST[0], WEST[0])), (straight_a, jnp.where(ox, WEST[0], EAST[0])),
+        (along_y.at[0], NORTH[0]), (along_y.at[1], SOUTH[0]),
+    )
+    for pair, d in straight:
         for p in range(2):
-            dst = along_y.at[n, p]
+            dst = pair.at[p]
             fetch_rows(SLOTS, lambda s, d=d: places[0, 0, d, s], [(rest.at[p], dst)])
             dst[...] = jnp.where(slot < tallies[0, 0, d], dst[...], 0.0)
 
@@ -227,7 +234,7 @@
 
 
 def kernel_fix(
-    places_h, tallies_h, home_h, hxb, hxa, hyb, hya, cw, cs, leave_b, leave_a, xb, xa, along_y, aq_in, at_in, table_in,
+    places_h, tallies_h, home_h, hxb, hxa, hyb, hya, cw, cs, leave_b, leave_a, straight_b, straight_a, xb, xa, along_y, aq_in, at_in, table_in,
     aq, at, table, send_b, send_a, rest_b, rest_a, got, places, tallies, home, sems,
 ):
     lists = ((places_h, places), (tallies_h, tallies), (home_h, home))
@@ -253,15 +260,20 @@
     for c in copies:
         c.wait()
     slot = lax.broadcasted_iota(jnp.int32, (SLOTS, LEV), 0)
-    radii, rests = (leave_b, leave_a), (xb, xa)
+    radii, rests, straight = (leave_b, leave_a), (xb, xa), (straight_b, straight_a)
     for k, (send, n, d) in enumerate(gx_sends((send_b, send_a))):
         fetch_rows(SLOTS, lambda s, d=d: home[places[0, 0, d, s]], [(table, got)])
-        square = growth_base(radii[k // 3][n], rests[k // 3][3 + 2 * n]) + 20.0 * got[...]
+        if n == 0:
+            solute = straight[k // 3][1]
+            send[3], send[4] = straight[k // 3][0], solute
+        else:
+            solute = rests[k // 3][2 * n + 1]
+        square = growth_base(radii[k // 3][n], solute) + 20.0 * got[...]
         send[n] = jnp.where(slot < tallies[0, 0, d], root(jnp.maximum(square, 0.25)), 0.0)
     for p in range(2):
         steer(
             (rest_b, rest_a), lambda n, p=p: 2 * n + p, along_y[0, p], along_y[1, p],
-            lambda n, p=p: hxb[2 + 2 * n + p], lambda n, p=p: hxa[2 + 2 * n + p],
+            lambda n, p=p: hxb[2 * n + p], lambda n, p=p: hxa[2 * n + p],
         )
 
 
@@ -337,11 +349,11 @@
         c.wait()
 
 
-def kernel_arrive(rb, ra, mb, ma, yrb, yra, ymb, yma, out, buf, sems):
+def kernel_arrive(rb, ra, yrb, yra, ymb, yma, out, buf, sems):
     ox, oy = odd_x(), odd_y()
     copies = []
     for d, odd, one, two, n, skip in (
-        (0, ox, (ra, ma), (rb, mb), 0, 2), (1, ox, (rb, mb), (ra, ma), 0, 2),
+        (0, ox, (ra, ra), (rb, rb), 0, 3), (1, ox, (rb, rb), (ra, ra), 0, 3),
         *((NORTH[n], oy, (yra, yma), (yrb, ymb), n, 0) for n in range(3)),
         *((SOUTH[n], oy, (yrb, ymb), (yra, yma), n, 0) for n in range(3)),
     ):
@@ -402,25 +414,26 @@
     sums = vmem(LANES_ACC, ROWS, LEV)
     xb, xa, yb, ya, rest = call(
         kernel_send, "send_edges", 1, [ANY] * 5, [VM] * 5,
-        [vmem(8, CY, LEV)] * 2 + [vmem(2, CX, LEV)] * 2 + [vmem(2, NB, LEV)],
+        [vmem(6, CY, LEV)] * 2 + [vmem(2, CX, LEV)] * 2 + [vmem(2, NB, LEV)],
         [vmem(2, 2, CY, LEV), vmem(2, 2, CX, 8, LEV), places_s, tallies_s, dma(2, 2), dma(2, 2), dma(4)],
     )(q_h, t_h, places_h, tallies_h, parts)
     hxb = swapped(xb, "gx", 1)
     hxa = swapped(xa, "gx", 0)
     hyb = swapped(yb, "gy", 1)
     hya = swapped(ya, "gy", 0)
-    aq, at, table, cw, cs, radius, leave_b, leave_a, along_y = call(
-        kernel_advect, "advect", 6, [ANY] * 2 + [VM] + [ANY] * 5, [VM] * 9,
+    aq, at, table, cw, cs, radius, leave_b, leave_a, straight_b, straight_a, along_y = call(
+        kernel_advect, "advect", 6, [ANY] * 2 + [VM] + [ANY] * 5, [VM] * 11,
         [cells, cells, table_of, vmem(CY, LEV), vmem(CX, LEV), blocks, radii, radii,
-         vmem(2, 2, SLOTS, LEV)],
+         vmem(2, SLOTS, LEV), vmem(2, SLOTS, LEV), vmem(2, 2, SLOTS, LEV)],
         [cells] * 4 + [places_s, tallies_s, dma(4, CHUNKS), dma(3)],
     )(places_h, tallies_h, rest, *flat, parts)
     aq, at, table, rb, ra, ymb, yma = call(
-        kernel_fix, "fix_edges", 1, [ANY] * 3 + [VM] * 14, [VM] * 7,
-        [cells, cells, table_of, radii, radii, pairs, pairs],
+        kernel_fix, "fix_edges", 1, [ANY] * 3 + [VM] * 16, [VM] * 7,
+        [cells, cells, table_of, vmem(5, SLOTS, LEV), vmem(5, SLOTS, LEV), pairs, pairs],
         [vmem(SLOTS, LEV), places_s, tallies_s, pltpu.SMEM((NB,), jnp.int32), dma(3)],
-        {14: 0, 15: 1, 16: 2},
-    )(places_h, tallies_h, home_h, hxb, hxa, hyb, hya, cw, cs, leave_b, leave_a, xb, xa, along_y, aq, at, table)
+        {16: 0, 17: 1, 18: 2},
+    )(places_h, tallies_h, home_h, hxb, hxa, hyb, hya, cw, cs, leave_b, leave_a, straight_b, straight_a,
+      xb, xa, along_y, aq, at, table)
     rb = swapped(rb, "gx", 1)
     ra = swapped(ra, "gx", 0)
     ymb = swapped(ymb, "gy", 1)
@@ -438,9 +451,9 @@
         [hbm(ROWS, LEV), hbm(ROWS, LEV), sums], [cells, cells, dma(2, CHUNKS)], {4: 2},
     )(home, cond, aq, at, acc)
     arrived = call(
-        kernel_arrive, "arrive", 1, [VM] * 8, ANY, hbm(8, 3, SLOTS, LEV),
+        kernel_arrive, "arrive", 1, [VM] * 6, ANY, hbm(8, 3, SLOTS, LEV),
         [vmem(8, 3, SLOTS, LEV), dma(8)],
-    )(rb, ra, hxb, hxa, yrb, yra, ymb, yma)
+    )(rb, ra, yrb, yra, ymb, yma)
     incoming = arrived.transpose(0, 2, 1, 3)[None, None]
     shape = (CX, CY, LEV)
     return q_out.reshape(shape), t_out.reshape(shape), parts_out.transpose(1, 0, 2), incoming

time: 55.5 us -> 52.2 us (0.941)
  waiting for transfers between devices: 7.2 us -> 4.04 us
    ppermute x10, waiting for transfers between devices: 7.2 us -> 4.04 us  [swapped(): lax.ppermute(value, axis, [(i, (i + step[i]) % count) for i in range(coun...]
    pallas_call x1, Pallas kernels: 4.04 us -> 3.1 us  [body(): call(kernel_deposit, 'deposit', 4, [SM] + [VM] * 4, [ANY, ANY, VM], [hbm(...]
    pallas_call x1, Pallas kernels: 5.91 us -> 6.79 us  [body(): call(kernel_grow, 'grow', 6, [SM] * 3 + [VM] * 3, [ANY, VM, VM, VM], [hbm...]
  transfers between devices with their start and end apart: 10 -> 10, of which waited for: 1 -> 2; matrix products, arithmetic and copies ran while one was open for 0% -> 0% of each run, Pallas kernels for 26% -> 28%
where the time goes in v3:
time: 52.2 us; the launch traced here: 52.1 us
  starting transfers between devices  27.4 us (52%)
  Pallas kernels  19.9 us (38%)
  waiting for transfers between devices  4.04 us (8%)
  between operations  0.76 us (1%)
    ppermute x10, starting transfers between devices, swapped(): lax.ppermute(value, axis, [(i, (i + step[i]) % count) for i in range(coun...  27.4 us
    pallas_call x1, Pallas kernels, body(): call(kernel_grow, 'grow', 6, [SM] * 3 + [VM] * 3, [ANY, VM, VM, VM], [hbm...  6.79 us
    pallas_call x1, Pallas kernels, body(): call(kernel_advect, 'advect', 6, [ANY] * 2 + [VM] + [ANY] * 5, [VM] * 11,...  4.83 us
    ppermute x10, waiting for transfers between devices, swapped(): lax.ppermute(value, axis, [(i, (i + step[i]) % count) for i in range(coun...  4.04 us
    pallas_call x1, Pallas kernels, body(): call(kernel_deposit, 'deposit', 4, [SM] + [VM] * 4, [ANY, ANY, VM], [hbm(...  3.1 us
    pallas_call x1, Pallas kernels, body(): call(kernel_send, 'send_edges', 1, [ANY] * 5, [VM] * 5, [vmem(6, CY, LEV)...  2.46 us
    pallas_call x1, Pallas kernels, body(): call(kernel_fix, 'fix_edges', 1, [ANY] * 3 + [VM] * 16, [VM] * 7, [cells,...  1.69 us
  transfers between devices with their start and end apart: 10, of which 2 were waited for; matrix products, arithmetic and copies ran while one was open for 0% of the time, Pallas kernels for 28%

profile of v3, /device:TPU:1, one launch (start us, length us, event | category | flops | bytes accessed | tf_op | source)
XLA Modules:
  0.0 52.1 jit_solution(18431291308213553324)
XLA Ops:
  0.6 2.5 %send_edges.1 = (f32[6,64,128]{2,1,0:T(8,128)S(1)}, f32[6,64,128]{2,1,0:T(8,128)S(1)}, f32[2,32,128]{2,1,0:T(8,128)S(1)}, f32[2,32,128]{2,1,0:T(8,128)S(1)}, f32[2,2048,128]{2,1,0:T(8,128)S(1)}) custom-call(f32[32,64,128]{2,1,0:T(8,128)} %q_h.1, f32[32,64,128]{2,1,0:T(8,128)} %t_h.1, s32[1,1,8,64]{3,2,1,0:T(8,128)} %places.1, s32[1,1,8]{2,1,0:T(1,128)} %tallies.1, ...), custom_call_target="tpu_custom_call" | custom-call | bytes 3000000 | tf_op jit(solution)/shard_map/send_edges/pallas_call | solution.py:415
  3.1 12.5 %collective-permute-start = (f32[6,64,128]{2,1,0:T(8,128)S(1)}, f32[6,64,128]{2,1,0:T(8,128)S(1)}, u32[]{:S(2)}, u32[]{:S(2)}) collective-permute-start(f32[6,64,128]{2,1,0:T(8,128)S(1)} %get-tuple-element.35.xb), channel_id=1, source_target_pairs={{0,248},{8,16},{16,8},{24,32},{32,24},{40,48},{48,40},{56,64},{64,... | collective-permute-start | bytes 589832 | tf_op jit(solution)/shard_map/ppermute | solution.py:403
  15.6 0.0 collective-permute-start.1
  15.6 1.6 %collective-permute-start.2 = (f32[2,32,128]{2,1,0:T(8,128)S(1)}, f32[2,32,128]{2,1,0:T(8,128)S(1)}, u32[]{:S(2)}, u32[]{:S(2)}) collective-permute-start(f32[2,32,128]{2,1,0:T(8,128)S(1)} %get-tuple-element.37), channel_id=1, source_target_pairs={{0,7},{1,2},{2,1},{3,4},{4,3},{5,6},{6,5},{7,0},{8,15},{9,10},{10,... | collective-permute-start | bytes 98312 | tf_op jit(solution)/shard_map/ppermute | solution.py:403
  17.1 0.5 collective-permute-start.3
  17.6 4.8 %advect.1 = (f32[2048,128]{1,0:T(8,128)S(1)}, f32[2048,128]{1,0:T(8,128)S(1)}, f32[4096,128]{1,0:T(8,128)S(1)}, f32[64,128]{1,0:T(8,128)S(1)}, f32[32,128]{1,0:T...) custom-call(s32[1,1,8,64]{3,2,1,0:T(8,128)} %places.1, ...), custom_call_target="tpu_custom_call" | custom-call | bytes 18000000 | tf_op jit(solution)/shard_map/advect/pallas_call | solution.py:424
  22.4 0.0 copy-start
  22.5 0.0 copy-start.1
  22.5 0.0 copy-start.2
  22.5 3.9 %collective-permute-done.2.hyb = f32[2,32,128]{2,1,0:T(8,128)S(1)} collective-permute-done((f32[2,32,128]{2,1,0:T(8,128)S(1)}, f32[2,32,128]{2,1,0:T(8,128)S(1)}, u32[]{:S(2)}, u32[]{:S(2)}) %collective-permute-start.2) | collective-permute-done | bytes 32800 | tf_op jit(solution)/shard_map/ppermute | solution.py:403
  26.4 0.0 collective-permute-done.3.hya
  26.4 0.0 collective-permute-done.hxb
  26.4 1.7 %fix_edges.1 = (f32[2048,128]{1,0:T(8,128)S(1)}, f32[2048,128]{1,0:T(8,128)S(1)}, f32[4096,128]{1,0:T(8,128)S(1)}, f32[5,64,128]{2,1,0:T(8,128)S(1)}, f32[5,64,1...) custom-call(s32[1,1,8,64]{3,2,1,0:T(8,128)} %places.1, ...), custom_call_target="tpu_custom_call", output_to_operand_aliasing={{0}: (16, {}), {1}: (17, {}), {2}: (18, {})} | custom-call | bytes 3000000 | tf_op jit(solution)/shard_map/fix_edges/pallas_call | solution.py:430
  28.1 7.7 %collective-permute-start.4 = (f32[5,64,128]{2,1,0:T(8,128)S(1)}, f32[5,64,128]{2,1,0:T(8,128)S(1)}, u32[]{:S(2)}, u32[]{:S(2)}) collective-permute-start(f32[5,64,128]{2,1,0:T(8,128)S(1)} %get-tuple-element.59), channel_id=1, source_target_pairs={{0,248},{8,16},{16,8},{24,32},{32,24},{40,48},{48,40},{56,64},{64,... | collective-permute-start | bytes 491528 | tf_op jit(solution)/shard_map/ppermute | solution.py:403
  35.8 0.0 collective-permute-start.5
  35.8 2.5 %collective-permute-start.8 = (f32[6,64,128]{2,1,0:T(8,128)S(1)}, f32[6,64,128]{2,1,0:T(8,128)S(1)}, u32[]{:S(2)}, u32[]{:S(2)}) collective-permute-start(f32[6,64,128]{2,1,0:T(8,128)S(1)} %get-tuple-element.64), channel_id=1, source_target_pairs={{0,7},{1,2},{2,1},{3,4},{4,3},{5,6},{6,5},{7,0},{8,15},{9,10},{10,... | collective-permute-start | bytes 589832 | tf_op jit(solution)/shard_map/ppermute | solution.py:403
  38.3 6.8 %grow.1 = (f32[3,2048,128]{2,1,0:T(8,128)}, f32[2048,128]{1,0:T(8,128)S(1)}, f32[2,64,128]{2,1,0:T(8,128)S(1)}, f32[4,2048,128]{2,1,0:T(8,128)S(1)}) custom-call(s32[1,1,8,64]{3,2,1,0:T(8,128)S(1)} %copy-done.1, s32[1,1,8]{2,1,0:T(1,128)S(1)} %copy-done.2, s32[2048]{0:T(1024)S(1)} %copy-done, f32[4096,128]{1,0:T(8,128)S(1)} %get-tuple-element.50.table, ...), custom_call_target="tpu_custom_call" | custom-call | bytes 18000000 | tf_op jit(solution)/shard_map/grow/pallas_call | solution.py:441
  45.1 0.1 collective-permute-done.4.rb
  45.2 0.0 collective-permute-done.5.ra
  45.2 0.1 collective-permute-start.6
  45.3 2.6 %collective-permute-start.7 = (f32[3,64,128]{2,1,0:T(8,128)S(1)}, f32[3,64,128]{2,1,0:T(8,128)S(1)}, u32[]{:S(2)}, u32[]{:S(2)}) collective-permute-start(f32[3,64,128]{2,1,0:T(8,128)S(1)} %get-tuple-element.63), channel_id=1, source_target_pairs={{0,1},{1,0},{2,3},{3,2},{4,5},{5,4},{6,7},{7,6},{8,9},{9,8},{10,11... | collective-permute-start | bytes 294920 | tf_op jit(solution)/shard_map/ppermute | solution.py:403
  48.0 3.1 %deposit.1 = (f32[2048,128]{1,0:T(8,128)}, f32[2048,128]{1,0:T(8,128)}, f32[4,2048,128]{2,1,0:T(8,128)S(1)}) custom-call(s32[2048]{0:T(1024)S(1)} %copy-done, f32[2048,128]{1,0:T(8,128)S(1)} %get-tuple-element.52.cond, f32[2048,128]{1,0:T(8,128)S(1)} %get-tuple-element.53.aq, f32[2048,128]{1,0:T(8,128)S(1)} %get-tuple-element.54.at, ...), custom_call_target="tpu_custom_call", output_to_operand_aliasing={{2}: (4, {})} | custom-call | bytes 12000000 | tf_op jit(solution)/shard_map/deposit/pallas_call | solution.py:449
  51.1 0.0 collective-permute-done.8.ymb
  51.1 1.0 %arrive.1 = f32[8,3,64,128]{3,2,1,0:T(8,128)} custom-call(f32[5,64,128]{2,1,0:T(8,128)S(1)} %collective-permute-done.4.rb, f32[5,64,128]{2,1,0:T(8,128)S(1)} %collective-permute-done.5.ra, f32[3,64,128]{2,1,0:T(8,128)S(1)} %collective-permute-done.6.yrb, f32[3,64,128]{2,1,0:T(8,128)S(1)} %collective-permute-done.7.yra, ...), custom_call_target="tpu_custom_call" | custom-call | bytes 3000000 | tf_op jit(solution)/shard_map/arrive/pallas_call | solution.py:453
  (9 shorter events, 0.0 us)
Async XLA Ops:
  3.1 23.3 %collective-permute-start = (f32[6,64,128]{2,1,0:T(8,128)S(1)}, f32[6,64,128]{2,1,0:T(8,128)S(1)}, u32[]{:S(2)}, u32[]{:S(2)}) collective-permute-start(f32[6,64,128]{2,1,0:T(8,128)S(1)} %get-tuple-element.35.xb), channel_id=1, source_target_pairs={{0,248},{8,16},{16,8},{24,32},{32,24},{40,48},{48,40},{56,64},{64,... | collective-permute-start | bytes 589832 | tf_op jit(solution)/shard_map/ppermute | solution.py:403
  15.6 10.8 %collective-permute-start.1 = (f32[6,64,128]{2,1,0:T(8,128)S(1)}, f32[6,64,128]{2,1,0:T(8,128)S(1)}, u32[]{:S(2)}, u32[]{:S(2)}) collective-permute-start(f32[6,64,128]{2,1,0:T(8,128)S(1)} %get-tuple-element.36.xa), channel_id=1, source_target_pairs={{0,8},{8,0},{16,24},{24,16},{32,40},{40,32},{48,56},{56,48},{64,72... | collective-permute-start | bytes 589832 | tf_op jit(solution)/shard_map/ppermute | solution.py:403
  15.6 10.8 %collective-permute-start.2 = (f32[2,32,128]{2,1,0:T(8,128)S(1)}, f32[2,32,128]{2,1,0:T(8,128)S(1)}, u32[]{:S(2)}, u32[]{:S(2)}) collective-permute-start(f32[2,32,128]{2,1,0:T(8,128)S(1)} %get-tuple-element.37), channel_id=1, source_target_pairs={{0,7},{1,2},{2,1},{3,4},{4,3},{5,6},{6,5},{7,0},{8,15},{9,10},{10,... | collective-permute-start | bytes 98312 | tf_op jit(solution)/shard_map/ppermute | solution.py:403
  17.1 9.2 %collective-permute-start.3 = (f32[2,32,128]{2,1,0:T(8,128)S(1)}, f32[2,32,128]{2,1,0:T(8,128)S(1)}, u32[]{:S(2)}, u32[]{:S(2)}) collective-permute-start(f32[2,32,128]{2,1,0:T(8,128)S(1)} %get-tuple-element.38), channel_id=1, source_target_pairs={{0,1},{1,0},{2,3},{3,2},{4,5},{5,4},{6,7},{7,6},{8,9},{9,8},{10,11... | collective-permute-start | bytes 98312 | tf_op jit(solution)/shard_map/ppermute | solution.py:403
  22.4 15.8 %copy-start = (s32[2048]{0:T(1024)S(1)}, s32[2048]{0:T(1024)}, u32[]{:S(2)}) copy-start(s32[2048]{0:T(1024)} %home.3) | copy-start | bytes 24580
  22.5 15.8 %copy-start.1 = (s32[1,1,8,64]{3,2,1,0:T(8,128)S(1)}, s32[1,1,8,64]{3,2,1,0:T(8,128)}, u32[]{:S(2)}) copy-start(s32[1,1,8,64]{3,2,1,0:T(8,128)} %places.1) | copy-start | bytes 6148
  22.5 15.8 %copy-start.2 = (s32[1,1,8]{2,1,0:T(1,128)S(1)}, s32[1,1,8]{2,1,0:T(1,128)}, u32[]{:S(2)}) copy-start(s32[1,1,8]{2,1,0:T(1,128)} %tallies.1) | copy-start | bytes 100
  28.1 17.1 %collective-permute-start.4 = (f32[5,64,128]{2,1,0:T(8,128)S(1)}, f32[5,64,128]{2,1,0:T(8,128)S(1)}, u32[]{:S(2)}, u32[]{:S(2)}) collective-permute-start(f32[5,64,128]{2,1,0:T(8,128)S(1)} %get-tuple-element.59), channel_id=1, source_target_pairs={{0,248},{8,16},{16,8},{24,32},{32,24},{40,48},{48,40},{56,64},{64,... | collective-permute-start | bytes 491528 | tf_op jit(solution)/shard_map/ppermute | solution.py:403
  35.8 9.4 %collective-permute-start.5 = (f32[5,64,128]{2,1,0:T(8,128)S(1)}, f32[5,64,128]{2,1,0:T(8,128)S(1)}, u32[]{:S(2)}, u32[]{:S(2)}) collective-permute-start(f32[5,64,128]{2,1,0:T(8,128)S(1)} %get-tuple-element.60), channel_id=1, source_target_pairs={{0,8},{8,0},{16,24},{24,16},{32,40},{40,32},{48,56},{56,48},{64,72... | collective-permute-start | bytes 491528 | tf_op jit(solution)/shard_map/ppermute | solution.py:403
  35.8 15.3 %collective-permute-start.8 = (f32[6,64,128]{2,1,0:T(8,128)S(1)}, f32[6,64,128]{2,1,0:T(8,128)S(1)}, u32[]{:S(2)}, u32[]{:S(2)}) collective-permute-start(f32[6,64,128]{2,1,0:T(8,128)S(1)} %get-tuple-element.64), channel_id=1, source_target_pairs={{0,7},{1,2},{2,1},{3,4},{4,3},{5,6},{6,5},{7,0},{8,15},{9,10},{10,... | collective-permute-start | bytes 589832 | tf_op jit(solution)/shard_map/ppermute | solution.py:403
  38.2 12.8 %collective-permute-start.9 = (f32[6,64,128]{2,1,0:T(8,128)S(1)}, f32[6,64,128]{2,1,0:T(8,128)S(1)}, u32[]{:S(2)}, u32[]{:S(2)}) collective-permute-start(f32[6,64,128]{2,1,0:T(8,128)S(1)} %get-tuple-element.65), channel_id=1, source_target_pairs={{0,1},{1,0},{2,3},{3,2},{4,5},{5,4},{6,7},{7,6},{8,9},{9,8},{10,11... | collective-permute-start | bytes 589832 | tf_op jit(solution)/shard_map/ppermute | solution.py:403
  45.2 5.9 %collective-permute-start.6 = (f32[3,64,128]{2,1,0:T(8,128)S(1)}, f32[3,64,128]{2,1,0:T(8,128)S(1)}, u32[]{:S(2)}, u32[]{:S(2)}) collective-permute-start(f32[3,64,128]{2,1,0:T(8,128)S(1)} %get-tuple-element.62), channel_id=1, source_target_pairs={{0,7},{1,2},{2,1},{3,4},{4,3},{5,6},{6,5},{7,0},{8,15},{9,10},{10,... | collective-permute-start | bytes 294920 | tf_op jit(solution)/shard_map/ppermute | solution.py:403
  45.3 5.8 %collective-permute-start.7 = (f32[3,64,128]{2,1,0:T(8,128)S(1)}, f32[3,64,128]{2,1,0:T(8,128)S(1)}, u32[]{:S(2)}, u32[]{:S(2)}) collective-permute-start(f32[3,64,128]{2,1,0:T(8,128)S(1)} %get-tuple-element.63), channel_id=1, source_target_pairs={{0,1},{1,0},{2,3},{3,2},{4,5},{5,4},{6,7},{7,6},{8,9},{9,8},{10,11... | collective-permute-start | bytes 294920 | tf_op jit(solution)/shard_map/ppermute | solution.py:403

commit v4 on v3

--- a/solution.py
+++ b/solution.py
@@ -15,7 +15,6 @@
 CROWS = ROWS // CHUNKS
 LANES_ACC = 4
 UNROLL = 8
-FIRST = 1536
 POWER = 17.27 * (273.15 - 35.86) * math.log2(math.e)
 SHIFT = 17.27 * math.log2(math.e) + math.log2(3.8)
 F32 = jnp.float32
@@ -172,7 +171,7 @@
 
 def kernel_advect(
     places_h, tallies_h, rest, q_h, t_h, we_h, wn_h, parts_h,
-    aq, at, table, cw, cs, radius, leave_b, leave_a, straight_b, straight_a, along_y,
+    aq, at, table, cw, cs, radius, base, acc, leave_b, leave_a, straight_b, straight_a, along_y,
     qv, tv, wev, wnv, places, tallies, sems, psem,
 ):
     copies = [
@@ -187,8 +186,17 @@
     cs[...] = wnv[pl.ds(0, CX, stride=CY)] + 0.1
     for c in copies:
         c.wait()
+
+    def prepare(g, _):
+        rows = pl.ds(pl.multiple_of(g * 64, 64), 64)
+        base[rows] = growth_base(radius[rows], rest[1, rows])
+        for k in range(LANES_ACC):
+            acc[k, rows] = jnp.zeros((64, LEV), F32)
+        return 0
+
+    lax.fori_loop(0, NB // 64, prepare, 0, unroll=2)
     for leave, n, d in gx_sends((leave_b, leave_a)):
-        fetch_rows(SLOTS, lambda s, d=d: places[0, 0, d, s], [(radius, leave.at[n])])
+        fetch_rows(SLOTS, lambda s, d=d: places[0, 0, d, s], [(base, leave.at[n])])
     slot = lax.broadcasted_iota(jnp.int32, (SLOTS, LEV), 0)
     ox = odd_x()
     straight = (
@@ -234,7 +242,7 @@
 
 
 def kernel_fix(
-    places_h, tallies_h, home_h, hxb, hxa, hyb, hya, cw, cs, leave_b, leave_a, straight_b, straight_a, xb, xa, along_y, aq_in, at_in, table_in,
+    places_h, tallies_h, home_h, hxb, hxa, hyb, hya, cw, cs, leave_b, leave_a, straight_b, straight_a, along_y, aq_in, at_in, table_in,
     aq, at, table, send_b, send_a, rest_b, rest_a, got, places, tallies, home, sems,
 ):
     lists = ((places_h, places), (tallies_h, tallies), (home_h, home))
@@ -260,15 +268,12 @@
     for c in copies:
         c.wait()
     slot = lax.broadcasted_iota(jnp.int32, (SLOTS, LEV), 0)
-    radii, rests, straight = (leave_b, leave_a), (xb, xa), (straight_b, straight_a)
+    bases, straight = (leave_b, leave_a), (straight_b, straight_a)
     for k, (send, n, d) in enumerate(gx_sends((send_b, send_a))):
         fetch_rows(SLOTS, lambda s, d=d: home[places[0, 0, d, s]], [(table, got)])
         if n == 0:
-            solute = straight[k // 3][1]
-            send[3], send[4] = straight[k // 3][0], solute
-        else:
-            solute = rests[k // 3][2 * n + 1]
-        square = growth_base(radii[k // 3][n], solute) + 20.0 * got[...]
+            send[3], send[4] = straight[k // 3][0], straight[k // 3][1]
+        square = bases[k // 3][n] + 20.0 * got[...]
         send[n] = jnp.where(slot < tallies[0, 0, d], root(jnp.maximum(square, 0.25)), 0.0)
     for p in range(2):
         steer(
@@ -277,7 +282,7 @@
         )
 
 
-def kernel_grow(places, tallies, home, table, radius, rest, parts_out, cond, ahead, acc, got, new_r, sems, psem):
+def kernel_grow(places, tallies, home, table, radius, rest, base, acc_in, parts_out, ahead, acc, cond, got, new_r, sems, psem):
     copies = [pltpu.make_async_copy(rest.at[p], parts_out.at[1 + p], psem.at[p]) for p in range(2)]
     for c in copies:
         c.start()
@@ -290,7 +295,7 @@
             here = pl.ds(pl.multiple_of(g * 64, 64), 64)
             rows = pl.ds(pl.multiple_of(k * per + g * 64, 64), 64)
             r, m = radius[rows], rest[0, rows]
-            square = growth_base(r, rest[1, rows]) + 20.0 * got[k % 2, here]
+            square = base[rows] + 20.0 * got[k % 2, here]
             square = jnp.maximum(square, 0.25)
             new = root(square)
             new_r[rows] = new
@@ -309,24 +314,16 @@
         dst = ahead.at[n]
         fetch_rows(SLOTS, lambda s, d=d: places[0, 0, d, s], [(new_r, dst)])
         dst[...] = jnp.where(slot < tallies[0, 0, d], dst[...], 0.0)
-
-    def clear(g, _):
-        for k in range(LANES_ACC):
-            acc[k, pl.ds(pl.multiple_of(g * 128, 128), 128)] = jnp.zeros((128, LEV), F32)
-        return 0
-
-    lax.fori_loop(0, ROWS // 128, clear, 0)
-    scatter_rows(home, cond, acc, 0, FIRST)
+    scatter_rows(home, cond, acc, 0, NB)
     for c in outs + copies:
         c.wait()
 
 
-def kernel_forward(ahead, rb, ra, yb, ya):
+def kernel_forward(ahead, ra, rb, yb, ya):
     steer((yb, ya), lambda n: n, ahead[0], ahead[1], lambda n: rb[n], lambda n: ra[n])
 
 
-def kernel_deposit(home, cond, aq, at, acc_in, q_out, t_out, acc, qo, to, sems):
-    scatter_rows(home, cond, acc, FIRST, NB)
+def kernel_deposit(aq, at, acc, q_out, t_out, qo, to, sems):
     outs = []
     for j in range(CHUNKS):
 
@@ -349,7 +346,7 @@
         c.wait()
 
 
-def kernel_arrive(rb, ra, yrb, yra, ymb, yma, out, buf, sems):
+def kernel_arrive(ra, rb, yrb, yra, ymb, yma, out, buf, sems):
     ox, oy = odd_x(), odd_y()
     copies = []
     for d, odd, one, two, n, skip in (
@@ -421,39 +418,39 @@
     hxa = swapped(xa, "gx", 0)
     hyb = swapped(yb, "gy", 1)
     hya = swapped(ya, "gy", 0)
-    aq, at, table, cw, cs, radius, leave_b, leave_a, straight_b, straight_a, along_y = call(
-        kernel_advect, "advect", 6, [ANY] * 2 + [VM] + [ANY] * 5, [VM] * 11,
-        [cells, cells, table_of, vmem(CY, LEV), vmem(CX, LEV), blocks, radii, radii,
+    aq, at, table, cw, cs, radius, base, acc, leave_b, leave_a, straight_b, straight_a, along_y = call(
+        kernel_advect, "advect", 6, [ANY] * 2 + [VM] + [ANY] * 5, [VM] * 13,
+        [cells, cells, table_of, vmem(CY, LEV), vmem(CX, LEV), blocks, blocks, sums, radii, radii,
          vmem(2, SLOTS, LEV), vmem(2, SLOTS, LEV), vmem(2, 2, SLOTS, LEV)],
         [cells] * 4 + [places_s, tallies_s, dma(4, CHUNKS), dma(3)],
     )(places_h, tallies_h, rest, *flat, parts)
     aq, at, table, rb, ra, ymb, yma = call(
-        kernel_fix, "fix_edges", 1, [ANY] * 3 + [VM] * 16, [VM] * 7,
+        kernel_fix, "fix_edges", 1, [ANY] * 3 + [VM] * 14, [VM] * 7,
         [cells, cells, table_of, vmem(5, SLOTS, LEV), vmem(5, SLOTS, LEV), pairs, pairs],
         [vmem(SLOTS, LEV), places_s, tallies_s, pltpu.SMEM((NB,), jnp.int32), dma(3)],
-        {16: 0, 17: 1, 18: 2},
-    )(places_h, tallies_h, home_h, hxb, hxa, hyb, hya, cw, cs, leave_b, leave_a, straight_b, straight_a,
-      xb, xa, along_y, aq, at, table)
+        {14: 0, 15: 1, 16: 2},
+    )(places_h, tallies_h, home_h, hxb, hxa, hyb, hya, cw, cs, leave_b, leave_a, straight_b, straight_a, along_y,
+      aq, at, table)
     rb = swapped(rb, "gx", 1)
     ra = swapped(ra, "gx", 0)
     ymb = swapped(ymb, "gy", 1)
     yma = swapped(yma, "gy", 0)
-    parts_out, cond, ahead, acc = call(
-        kernel_grow, "grow", 6, [SM] * 3 + [VM] * 3, [ANY, VM, VM, VM],
-        [hbm(3, NB, LEV), blocks, vmem(2, SLOTS, LEV), sums],
-        [vmem(2, NB // CHUNKS, LEV), blocks, dma(CHUNKS), dma(2)],
-    )(places, tallies, home, table, radius, rest)
-    yb, ya = call(kernel_forward, "forward", 1, [VM] * 3, [VM] * 2, [radii, radii], [])(ahead, rb, ra)
+    parts_out, ahead, acc = call(
+        kernel_grow, "grow", 6, [SM] * 3 + [VM] * 5, [ANY, VM, VM],
+        [hbm(3, NB, LEV), vmem(2, SLOTS, LEV), sums],
+        [blocks, vmem(2, NB // CHUNKS, LEV), blocks, dma(CHUNKS), dma(2)], {7: 2},
+    )(places, tallies, home, table, radius, rest, base, acc)
+    yb, ya = call(kernel_forward, "forward", 1, [VM] * 3, [VM] * 2, [radii, radii], [])(ahead, ra, rb)
     yrb = swapped(yb, "gy", 1)
     yra = swapped(ya, "gy", 0)
-    q_out, t_out, _ = call(
-        kernel_deposit, "deposit", 4, [SM] + [VM] * 4, [ANY, ANY, VM],
-        [hbm(ROWS, LEV), hbm(ROWS, LEV), sums], [cells, cells, dma(2, CHUNKS)], {4: 2},
-    )(home, cond, aq, at, acc)
+    q_out, t_out = call(
+        kernel_deposit, "deposit", 4, [VM] * 3, [ANY, ANY],
+        [hbm(ROWS, LEV), hbm(ROWS, LEV)], [cells, cells, dma(2, CHUNKS)],
+    )(aq, at, acc)
     arrived = call(
         kernel_arrive, "arrive", 1, [VM] * 6, ANY, hbm(8, 3, SLOTS, LEV),
         [vmem(8, 3, SLOTS, LEV), dma(8)],
-    )(rb, ra, yrb, yra, ymb, yma)
+    )(ra, rb, yrb, yra, ymb, yma)
     incoming = arrived.transpose(0, 2, 1, 3)[None, None]
     shape = (CX, CY, LEV)
     return q_out.reshape(shape), t_out.reshape(shape), parts_out.transpose(1, 0, 2), incoming

time: 52.2 us -> 51 us (0.977)
  Pallas kernels: 19.9 us -> 19 us
  waiting for transfers between devices: 4.04 us -> 3.45 us
    pallas_call x4, Pallas kernels: 16.4 us -> 15.6 us  [the longest x1 7.13 us: body(): call(kernel_grow, 'grow', 6, [SM] * 3 + [VM] * 5, [ANY, VM, VM], [hbm(3,...]
    ppermute x10, waiting for transfers between devices: 4.04 us -> 3.45 us  [swapped(): lax.ppermute(value, axis, [(i, (i + step[i]) % count) for i in range(coun...]
  transfers between devices with their start and end apart: 10 -> 10, of which waited for: 2 -> 1; matrix products, arithmetic and copies ran while one was open for 0% -> 0% of each run, Pallas kernels for 28% -> 27%
where the time goes in v4:
time: 51 us; the launch traced here: 50.9 us
  starting transfers between devices  27.6 us (54%)
  Pallas kernels  19 us (37%)
  waiting for transfers between devices  3.45 us (7%)
  between operations  0.79 us (2%)
    ppermute x10, starting transfers between devices, swapped(): lax.ppermute(value, axis, [(i, (i + step[i]) % count) for i in range(coun...  27.6 us
    pallas_call x1, Pallas kernels, body(): call(kernel_grow, 'grow', 6, [SM] * 3 + [VM] * 5, [ANY, VM, VM], [hbm(3,...  7.13 us
    pallas_call x1, Pallas kernels, body(): call(kernel_advect, 'advect', 6, [ANY] * 2 + [VM] + [ANY] * 5, [VM] * 13,...  5.3 us
    ppermute x10, waiting for transfers between devices, swapped(): lax.ppermute(value, axis, [(i, (i + step[i]) % count) for i in range(coun...  3.45 us
    pallas_call x1, Pallas kernels, body(): call(kernel_send, 'send_edges', 1, [ANY] * 5, [VM] * 5, [vmem(6, CY, LEV)...  2.46 us
    pallas_call x1, Pallas kernels, body(): call(kernel_fix, 'fix_edges', 1, [ANY] * 3 + [VM] * 14, [VM] * 7, [cells,...  1.65 us
    pallas_call x1, Pallas kernels, body(): call(kernel_deposit, 'deposit', 4, [VM] * 3, [ANY, ANY], [hbm(ROWS, LEV),...  1.49 us
  transfers between devices with their start and end apart: 10, of which 1 were waited for; matrix products, arithmetic and copies ran while one was open for 0% of the time, Pallas kernels for 27%

profile of v4, /device:TPU:1, one launch (start us, length us, event | category | flops | bytes accessed | tf_op | source)
XLA Modules:
  0.0 50.9 jit_solution(11726623946822237437)
XLA Ops:
  0.6 2.5 %send_edges.1 = (f32[6,64,128]{2,1,0:T(8,128)S(1)}, f32[6,64,128]{2,1,0:T(8,128)S(1)}, f32[2,32,128]{2,1,0:T(8,128)S(1)}, f32[2,32,128]{2,1,0:T(8,128)S(1)}, f32[2,2048,128]{2,1,0:T(8,128)S(1)}) custom-call(f32[32,64,128]{2,1,0:T(8,128)} %q_h.1, f32[32,64,128]{2,1,0:T(8,128)} %t_h.1, s32[1,1,8,64]{3,2,1,0:T(8,128)} %places.1, s32[1,1,8]{2,1,0:T(1,128)} %tallies.1, ...), custom_call_target="tpu_custom_call" | custom-call | bytes 3000000 | tf_op jit(solution)/shard_map/send_edges/pallas_call | solution.py:412
  3.1 12.5 %collective-permute-start = (f32[6,64,128]{2,1,0:T(8,128)S(1)}, f32[6,64,128]{2,1,0:T(8,128)S(1)}, u32[]{:S(2)}, u32[]{:S(2)}) collective-permute-start(f32[6,64,128]{2,1,0:T(8,128)S(1)} %get-tuple-element.36), channel_id=1, source_target_pairs={{0,248},{8,16},{16,8},{24,32},{32,24},{40,48},{48,40},{56,64},{64,... | collective-permute-start | bytes 589832 | tf_op jit(solution)/shard_map/ppermute | solution.py:400
  15.6 1.6 %collective-permute-start.2 = (f32[2,32,128]{2,1,0:T(8,128)S(1)}, f32[2,32,128]{2,1,0:T(8,128)S(1)}, u32[]{:S(2)}, u32[]{:S(2)}) collective-permute-start(f32[2,32,128]{2,1,0:T(8,128)S(1)} %get-tuple-element.38), channel_id=1, source_target_pairs={{0,7},{1,2},{2,1},{3,4},{4,3},{5,6},{6,5},{7,0},{8,15},{9,10},{10,... | collective-permute-start | bytes 98312 | tf_op jit(solution)/shard_map/ppermute | solution.py:400
  17.1 0.5 collective-permute-start.3
  17.6 5.3 %advect.1 = (f32[2048,128]{1,0:T(8,128)S(1)}, f32[2048,128]{1,0:T(8,128)S(1)}, f32[4096,128]{1,0:T(8,128)S(1)}, f32[64,128]{1,0:T(8,128)S(1)}, f32[32,128]{1,0:T...) custom-call(s32[1,1,8,64]{3,2,1,0:T(8,128)} %places.1, ...), custom_call_target="tpu_custom_call" | custom-call | bytes 18000000 | tf_op jit(solution)/shard_map/advect/pallas_call | solution.py:421
  22.9 0.0 copy-start
  22.9 0.0 copy-start.1
  22.9 0.0 copy-start.2
  23.0 3.4 %collective-permute-done.2.hyb = f32[2,32,128]{2,1,0:T(8,128)S(1)} collective-permute-done((f32[2,32,128]{2,1,0:T(8,128)S(1)}, f32[2,32,128]{2,1,0:T(8,128)S(1)}, u32[]{:S(2)}, u32[]{:S(2)}) %collective-permute-start.2) | collective-permute-done | bytes 32800 | tf_op jit(solution)/shard_map/ppermute | solution.py:400
  26.4 0.0 collective-permute-done.3.hya
  26.4 0.0 collective-permute-done.hxb
  26.4 0.0 collective-permute-done.1.hxa
  26.4 1.7 %fix_edges.1 = (f32[2048,128]{1,0:T(8,128)S(1)}, f32[2048,128]{1,0:T(8,128)S(1)}, f32[4096,128]{1,0:T(8,128)S(1)}, f32[5,64,128]{2,1,0:T(8,128)S(1)}, f32[5,64,1...) custom-call(s32[1,1,8,64]{3,2,1,0:T(8,128)} %places.1, ...), custom_call_target="tpu_custom_call", output_to_operand_aliasing={{0}: (14, {}), {1}: (15, {}), {2}: (16, {})} | custom-call | bytes 3000000 | tf_op jit(solution)/shard_map/fix_edges/pallas_call | solution.py:427
  28.1 0.1 collective-permute-start.4
  28.2 7.7 %collective-permute-start.5 = (f32[5,64,128]{2,1,0:T(8,128)S(1)}, f32[5,64,128]{2,1,0:T(8,128)S(1)}, u32[]{:S(2)}, u32[]{:S(2)}) collective-permute-start(f32[5,64,128]{2,1,0:T(8,128)S(1)} %get-tuple-element.62), channel_id=1, source_target_pairs={{0,248},{8,16},{16,8},{24,32},{32,24},{40,48},{48,40},{56,64},{64,... | collective-permute-start | bytes 491528 | tf_op jit(solution)/shard_map/ppermute | solution.py:400
  35.8 2.5 %collective-permute-start.8 = (f32[6,64,128]{2,1,0:T(8,128)S(1)}, f32[6,64,128]{2,1,0:T(8,128)S(1)}, u32[]{:S(2)}, u32[]{:S(2)}) collective-permute-start(f32[6,64,128]{2,1,0:T(8,128)S(1)} %get-tuple-element.66), channel_id=1, source_target_pairs={{0,7},{1,2},{2,1},{3,4},{4,3},{5,6},{6,5},{7,0},{8,15},{9,10},{10,... | collective-permute-start | bytes 589832 | tf_op jit(solution)/shard_map/ppermute | solution.py:400
  38.3 7.1 %grow.1 = (f32[3,2048,128]{2,1,0:T(8,128)}, f32[2,64,128]{2,1,0:T(8,128)S(1)}, f32[4,2048,128]{2,1,0:T(8,128)S(1)}) custom-call(s32[1,1,8,64]{3,2,1,0:T(8,128)S(1)} %copy-done, s32[1,1,8]{2,1,0:T(1,128)S(1)} %copy-done.2, s32[2048]{0:T(1024)S(1)} %copy-done.1, f32[4096,128]{1,0:T(8,128)S(1)} %get-tuple-element.53.table, ...), custom_call_target="tpu_custom_call", output_to_operand_aliasing={{2}: (7, {})} | custom-call | bytes 18000000 | tf_op jit(solution)/shard_map/grow/pallas_call | solution.py:438
  45.5 0.0 collective-permute-done.5.rb
  45.5 0.1 collective-permute-start.6
  45.6 2.7 %collective-permute-start.7 = (f32[3,64,128]{2,1,0:T(8,128)S(1)}, f32[3,64,128]{2,1,0:T(8,128)S(1)}, u32[]{:S(2)}, u32[]{:S(2)}) collective-permute-start(f32[3,64,128]{2,1,0:T(8,128)S(1)} %get-tuple-element.65), channel_id=1, source_target_pairs={{0,1},{1,0},{2,3},{3,2},{4,5},{5,4},{6,7},{7,6},{8,9},{9,8},{10,11... | collective-permute-start | bytes 294920 | tf_op jit(solution)/shard_map/ppermute | solution.py:400
  48.4 1.5 %deposit.1 = (f32[2048,128]{1,0:T(8,128)}, f32[2048,128]{1,0:T(8,128)}) custom-call(f32[2048,128]{1,0:T(8,128)S(1)} %get-tuple-element.51.aq, f32[2048,128]{1,0:T(8,128)S(1)} %get-tuple-element.52.at, f32[4,2048,128]{2,1,0:T(8,128)S(1)} %get-tuple-element.57.acc), custom_call_target="tpu_custom_call" | custom-call | bytes 12000000 | tf_op jit(solution)/shard_map/deposit/pallas_call | solution.py:446
  49.9 0.0 collective-permute-done.9.yma
  49.9 0.0 collective-permute-done.6.yrb
  49.9 1.0 %arrive.1 = f32[8,3,64,128]{3,2,1,0:T(8,128)} custom-call(f32[5,64,128]{2,1,0:T(8,128)S(1)} %collective-permute-done.4.ra, f32[5,64,128]{2,1,0:T(8,128)S(1)} %collective-permute-done.5.rb, f32[3,64,128]{2,1,0:T(8,128)S(1)} %collective-permute-done.6.yrb, f32[3,64,128]{2,1,0:T(8,128)S(1)} %collective-permute-done.7.yra, ...), custom_call_target="tpu_custom_call" | custom-call | bytes 3000000 | tf_op jit(solution)/shard_map/arrive/pallas_call | solution.py:450
  (9 shorter events, 0.0 us)
Async XLA Ops:
  3.1 23.3 %collective-permute-start = (f32[6,64,128]{2,1,0:T(8,128)S(1)}, f32[6,64,128]{2,1,0:T(8,128)S(1)}, u32[]{:S(2)}, u32[]{:S(2)}) collective-permute-start(f32[6,64,128]{2,1,0:T(8,128)S(1)} %get-tuple-element.36), channel_id=1, source_target_pairs={{0,248},{8,16},{16,8},{24,32},{32,24},{40,48},{48,40},{56,64},{64,... | collective-permute-start | bytes 589832 | tf_op jit(solution)/shard_map/ppermute | solution.py:400
  15.6 10.8 %collective-permute-start.1 = (f32[6,64,128]{2,1,0:T(8,128)S(1)}, f32[6,64,128]{2,1,0:T(8,128)S(1)}, u32[]{:S(2)}, u32[]{:S(2)}) collective-permute-start(f32[6,64,128]{2,1,0:T(8,128)S(1)} %get-tuple-element.37), channel_id=1, source_target_pairs={{0,8},{8,0},{16,24},{24,16},{32,40},{40,32},{48,56},{56,48},{64,72... | collective-permute-start | bytes 589832 | tf_op jit(solution)/shard_map/ppermute | solution.py:400
  15.6 10.8 %collective-permute-start.2 = (f32[2,32,128]{2,1,0:T(8,128)S(1)}, f32[2,32,128]{2,1,0:T(8,128)S(1)}, u32[]{:S(2)}, u32[]{:S(2)}) collective-permute-start(f32[2,32,128]{2,1,0:T(8,128)S(1)} %get-tuple-element.38), channel_id=1, source_target_pairs={{0,7},{1,2},{2,1},{3,4},{4,3},{5,6},{6,5},{7,0},{8,15},{9,10},{10,... | collective-permute-start | bytes 98312 | tf_op jit(solution)/shard_map/ppermute | solution.py:400
  17.1 9.2 %collective-permute-start.3 = (f32[2,32,128]{2,1,0:T(8,128)S(1)}, f32[2,32,128]{2,1,0:T(8,128)S(1)}, u32[]{:S(2)}, u32[]{:S(2)}) collective-permute-start(f32[2,32,128]{2,1,0:T(8,128)S(1)} %get-tuple-element.39), channel_id=1, source_target_pairs={{0,1},{1,0},{2,3},{3,2},{4,5},{5,4},{6,7},{7,6},{8,9},{9,8},{10,11... | collective-permute-start | bytes 98312 | tf_op jit(solution)/shard_map/ppermute | solution.py:400
  22.9 15.4 %copy-start = (s32[1,1,8,64]{3,2,1,0:T(8,128)S(1)}, s32[1,1,8,64]{3,2,1,0:T(8,128)}, u32[]{:S(2)}) copy-start(s32[1,1,8,64]{3,2,1,0:T(8,128)} %places.1) | copy-start | bytes 6148
  22.9 15.4 %copy-start.1 = (s32[2048]{0:T(1024)S(1)}, s32[2048]{0:T(1024)}, u32[]{:S(2)}) copy-start(s32[2048]{0:T(1024)} %home.1) | copy-start | bytes 24580
  22.9 15.4 %copy-start.2 = (s32[1,1,8]{2,1,0:T(1,128)S(1)}, s32[1,1,8]{2,1,0:T(1,128)}, u32[]{:S(2)}) copy-start(s32[1,1,8]{2,1,0:T(1,128)} %tallies.1) | copy-start | bytes 100
  28.1 17.4 %collective-permute-start.4 = (f32[5,64,128]{2,1,0:T(8,128)S(1)}, f32[5,64,128]{2,1,0:T(8,128)S(1)}, u32[]{:S(2)}, u32[]{:S(2)}) collective-permute-start(f32[5,64,128]{2,1,0:T(8,128)S(1)} %get-tuple-element.61), channel_id=1, source_target_pairs={{0,8},{8,0},{16,24},{24,16},{32,40},{40,32},{48,56},{56,48},{64,72... | collective-permute-start | bytes 491528 | tf_op jit(solution)/shard_map/ppermute | solution.py:400
  28.2 17.3 %collective-permute-start.5 = (f32[5,64,128]{2,1,0:T(8,128)S(1)}, f32[5,64,128]{2,1,0:T(8,128)S(1)}, u32[]{:S(2)}, u32[]{:S(2)}) collective-permute-start(f32[5,64,128]{2,1,0:T(8,128)S(1)} %get-tuple-element.62), channel_id=1, source_target_pairs={{0,248},{8,16},{16,8},{24,32},{32,24},{40,48},{48,40},{56,64},{64,... | collective-permute-start | bytes 491528 | tf_op jit(solution)/shard_map/ppermute | solution.py:400
  35.8 14.0 %collective-permute-start.8 = (f32[6,64,128]{2,1,0:T(8,128)S(1)}, f32[6,64,128]{2,1,0:T(8,128)S(1)}, u32[]{:S(2)}, u32[]{:S(2)}) collective-permute-start(f32[6,64,128]{2,1,0:T(8,128)S(1)} %get-tuple-element.66), channel_id=1, source_target_pairs={{0,7},{1,2},{2,1},{3,4},{4,3},{5,6},{6,5},{7,0},{8,15},{9,10},{10,... | collective-permute-start | bytes 589832 | tf_op jit(solution)/shard_map/ppermute | solution.py:400
  38.3 11.6 %collective-permute-start.9 = (f32[6,64,128]{2,1,0:T(8,128)S(1)}, f32[6,64,128]{2,1,0:T(8,128)S(1)}, u32[]{:S(2)}, u32[]{:S(2)}) collective-permute-start(f32[6,64,128]{2,1,0:T(8,128)S(1)} %get-tuple-element.67), channel_id=1, source_target_pairs={{0,1},{1,0},{2,3},{3,2},{4,5},{5,4},{6,7},{7,6},{8,9},{9,8},{10,11... | collective-permute-start | bytes 589832 | tf_op jit(solution)/shard_map/ppermute | solution.py:400
  45.5 4.4 %collective-permute-start.6 = (f32[3,64,128]{2,1,0:T(8,128)S(1)}, f32[3,64,128]{2,1,0:T(8,128)S(1)}, u32[]{:S(2)}, u32[]{:S(2)}) collective-permute-start(f32[3,64,128]{2,1,0:T(8,128)S(1)} %get-tuple-element.64), channel_id=1, source_target_pairs={{0,7},{1,2},{2,1},{3,4},{4,3},{5,6},{6,5},{7,0},{8,15},{9,10},{10,... | collective-permute-start | bytes 294920 | tf_op jit(solution)/shard_map/ppermute | solution.py:400
  45.6 4.3 %collective-permute-start.7 = (f32[3,64,128]{2,1,0:T(8,128)S(1)}, f32[3,64,128]{2,1,0:T(8,128)S(1)}, u32[]{:S(2)}, u32[]{:S(2)}) collective-permute-start(f32[3,64,128]{2,1,0:T(8,128)S(1)} %get-tuple-element.65), channel_id=1, source_target_pairs={{0,1},{1,0},{2,3},{3,2},{4,5},{5,4},{6,7},{7,6},{8,9},{9,8},{10,11... | collective-permute-start | bytes 294920 | tf_op jit(solution)/shard_map/ppermute | solution.py:400

commit v5 on v4

--- a/solution.py
+++ b/solution.py
@@ -13,8 +13,8 @@
 SLOTS = 64
 CHUNKS = 8
 CROWS = ROWS // CHUNKS
-LANES_ACC = 4
-UNROLL = 8
+LANES_ACC = 8
+UNROLL = 4
 POWER = 17.27 * (273.15 - 35.86) * math.log2(math.e)
 SHIFT = 17.27 * math.log2(math.e) + math.log2(3.8)
 F32 = jnp.float32
@@ -289,7 +289,7 @@
     outs = []
     per = NB // CHUNKS
     for k in range(CHUNKS):
-        fetch_rows(per, lambda s, k=k: home[k * per + s], [(table, got.at[k % 2])])
+        fetch_rows(per, lambda s, k=k: home[k * per + s], [(table, got.at[k % 2])], 128)
 
         def grow(g, _, k=k):
             here = pl.ds(pl.multiple_of(g * 64, 64), 64)

time: 51 us -> 51 us (level)
  transfers between devices with their start and end apart: 10 -> 10, of which waited for: 1 -> 2; matrix products, arithmetic and copies ran while one was open for 0% -> 0% of each run, Pallas kernels for 27% -> 27%
where the time goes in v5:
time: 51 us; the launch traced here: 50.5 us
  starting transfers between devices  27.5 us (54%)
  Pallas kernels  18.9 us (37%)
  waiting for transfers between devices  3.33 us (7%)
  between operations  0.78 us (2%)
    ppermute x10, starting transfers between devices, swapped(): lax.ppermute(value, axis, [(i, (i + step[i]) % count) for i in range(coun...  27.5 us
    pallas_call x1, Pallas kernels, body(): call(kernel_grow, 'grow', 6, [SM] * 3 + [VM] * 5, [ANY, VM, VM], [hbm(3,...  6.75 us
    pallas_call x1, Pallas kernels, body(): call(kernel_advect, 'advect', 6, [ANY] * 2 + [VM] + [ANY] * 5, [VM] * 13,...  5.57 us
    ppermute x10, waiting for transfers between devices, swapped(): lax.ppermute(value, axis, [(i, (i + step[i]) % count) for i in range(coun...  3.33 us
    pallas_call x1, Pallas kernels, body(): call(kernel_send, 'send_edges', 1, [ANY] * 5, [VM] * 5, [vmem(6, CY, LEV)...  2.46 us
    pallas_call x1, Pallas kernels, body(): call(kernel_fix, 'fix_edges', 1, [ANY] * 3 + [VM] * 14, [VM] * 7, [cells,...  1.65 us
    pallas_call x1, Pallas kernels, body(): call(kernel_deposit, 'deposit', 4, [VM] * 3, [ANY, ANY], [hbm(ROWS, LEV),...  1.53 us
  transfers between devices with their start and end apart: 10, of which 2 were waited for; matrix products, arithmetic and copies ran while one was open for 0% of the time, Pallas kernels for 27%

profile of v5, /device:TPU:1, one launch (start us, length us, event | category | flops | bytes accessed | tf_op | source)
XLA Modules:
  0.0 50.5 jit_solution(10741885336747419248)
XLA Ops:
  0.6 2.5 %send_edges.1 = (f32[6,64,128]{2,1,0:T(8,128)S(1)}, f32[6,64,128]{2,1,0:T(8,128)S(1)}, f32[2,32,128]{2,1,0:T(8,128)S(1)}, f32[2,32,128]{2,1,0:T(8,128)S(1)}, f32[2,2048,128]{2,1,0:T(8,128)S(1)}) custom-call(f32[32,64,128]{2,1,0:T(8,128)} %q_h.1, f32[32,64,128]{2,1,0:T(8,128)} %t_h.1, s32[1,1,8,64]{3,2,1,0:T(8,128)} %places.1, s32[1,1,8]{2,1,0:T(1,128)} %tallies.1, ...), custom_call_target="tpu_custom_call" | custom-call | bytes 3000000 | tf_op jit(solution)/shard_map/send_edges/pallas_call | solution.py:412
  3.1 12.5 %collective-permute-start = (f32[6,64,128]{2,1,0:T(8,128)S(1)}, f32[6,64,128]{2,1,0:T(8,128)S(1)}, u32[]{:S(2)}, u32[]{:S(2)}) collective-permute-start(f32[6,64,128]{2,1,0:T(8,128)S(1)} %get-tuple-element.36), channel_id=1, source_target_pairs={{0,248},{8,16},{16,8},{24,32},{32,24},{40,48},{48,40},{56,64},{64,... | collective-permute-start | bytes 589832 | tf_op jit(solution)/shard_map/ppermute | solution.py:400
  15.6 0.0 collective-permute-start.1
  15.6 1.6 %collective-permute-start.2 = (f32[2,32,128]{2,1,0:T(8,128)S(1)}, f32[2,32,128]{2,1,0:T(8,128)S(1)}, u32[]{:S(2)}, u32[]{:S(2)}) collective-permute-start(f32[2,32,128]{2,1,0:T(8,128)S(1)} %get-tuple-element.38), channel_id=1, source_target_pairs={{0,7},{1,2},{2,1},{3,4},{4,3},{5,6},{6,5},{7,0},{8,15},{9,10},{10,... | collective-permute-start | bytes 98312 | tf_op jit(solution)/shard_map/ppermute | solution.py:400
  17.1 0.5 collective-permute-start.3
  17.6 5.6 %advect.1 = (f32[2048,128]{1,0:T(8,128)S(1)}, f32[2048,128]{1,0:T(8,128)S(1)}, f32[4096,128]{1,0:T(8,128)S(1)}, f32[64,128]{1,0:T(8,128)S(1)}, f32[32,128]{1,0:T...) custom-call(s32[1,1,8,64]{3,2,1,0:T(8,128)} %places.1, ...), custom_call_target="tpu_custom_call" | custom-call | bytes 18000000 | tf_op jit(solution)/shard_map/advect/pallas_call | solution.py:421
  23.2 0.0 copy-start
  23.2 0.0 copy-start.1
  23.2 0.0 copy-start.2
  23.2 3.2 %collective-permute-done.2.hyb = f32[2,32,128]{2,1,0:T(8,128)S(1)} collective-permute-done((f32[2,32,128]{2,1,0:T(8,128)S(1)}, f32[2,32,128]{2,1,0:T(8,128)S(1)}, u32[]{:S(2)}, u32[]{:S(2)}) %collective-permute-start.2) | collective-permute-done | bytes 32800 | tf_op jit(solution)/shard_map/ppermute | solution.py:400
  26.4 0.0 collective-permute-done.3.hya
  26.4 0.0 collective-permute-done.hxb
  26.4 1.6 %fix_edges.1 = (f32[2048,128]{1,0:T(8,128)S(1)}, f32[2048,128]{1,0:T(8,128)S(1)}, f32[4096,128]{1,0:T(8,128)S(1)}, f32[5,64,128]{2,1,0:T(8,128)S(1)}, f32[5,64,1...) custom-call(s32[1,1,8,64]{3,2,1,0:T(8,128)} %places.1, ...), custom_call_target="tpu_custom_call", output_to_operand_aliasing={{0}: (14, {}), {1}: (15, {}), {2}: (16, {})} | custom-call | bytes 3000000 | tf_op jit(solution)/shard_map/fix_edges/pallas_call | solution.py:427
  28.0 0.1 collective-permute-start.4
  28.1 7.7 %collective-permute-start.5 = (f32[5,64,128]{2,1,0:T(8,128)S(1)}, f32[5,64,128]{2,1,0:T(8,128)S(1)}, u32[]{:S(2)}, u32[]{:S(2)}) collective-permute-start(f32[5,64,128]{2,1,0:T(8,128)S(1)} %get-tuple-element.62), channel_id=1, source_target_pairs={{0,248},{8,16},{16,8},{24,32},{32,24},{40,48},{48,40},{56,64},{64,... | collective-permute-start | bytes 491528 | tf_op jit(solution)/shard_map/ppermute | solution.py:400
  35.8 2.5 %collective-permute-start.8 = (f32[6,64,128]{2,1,0:T(8,128)S(1)}, f32[6,64,128]{2,1,0:T(8,128)S(1)}, u32[]{:S(2)}, u32[]{:S(2)}) collective-permute-start(f32[6,64,128]{2,1,0:T(8,128)S(1)} %get-tuple-element.66), channel_id=1, source_target_pairs={{0,7},{1,2},{2,1},{3,4},{4,3},{5,6},{6,5},{7,0},{8,15},{9,10},{10,... | collective-permute-start | bytes 589832 | tf_op jit(solution)/shard_map/ppermute | solution.py:400
  38.3 6.8 %grow.1 = (f32[3,2048,128]{2,1,0:T(8,128)}, f32[2,64,128]{2,1,0:T(8,128)S(1)}, f32[8,2048,128]{2,1,0:T(8,128)S(1)}) custom-call(s32[1,1,8,64]{3,2,1,0:T(8,128)S(1)} %copy-done, s32[1,1,8]{2,1,0:T(1,128)S(1)} %copy-done.2, s32[2048]{0:T(1024)S(1)} %copy-done.1, f32[4096,128]{1,0:T(8,128)S(1)} %get-tuple-element.53.table, ...), custom_call_target="tpu_custom_call", output_to_operand_aliasing={{2}: (7, {})} | custom-call | bytes 18000000 | tf_op jit(solution)/shard_map/grow/pallas_call | solution.py:438
  45.1 0.2 collective-permute-done.5.rb
  45.3 0.1 collective-permute-start.6
  45.4 2.6 %collective-permute-start.7 = (f32[3,64,128]{2,1,0:T(8,128)S(1)}, f32[3,64,128]{2,1,0:T(8,128)S(1)}, u32[]{:S(2)}, u32[]{:S(2)}) collective-permute-start(f32[3,64,128]{2,1,0:T(8,128)S(1)} %get-tuple-element.65), channel_id=1, source_target_pairs={{0,1},{1,0},{2,3},{3,2},{4,5},{5,4},{6,7},{7,6},{8,9},{9,8},{10,11... | collective-permute-start | bytes 294920 | tf_op jit(solution)/shard_map/ppermute | solution.py:400
  48.0 1.5 %deposit.1 = (f32[2048,128]{1,0:T(8,128)}, f32[2048,128]{1,0:T(8,128)}) custom-call(f32[2048,128]{1,0:T(8,128)S(1)} %get-tuple-element.51.aq, f32[2048,128]{1,0:T(8,128)S(1)} %get-tuple-element.52.at, f32[8,2048,128]{2,1,0:T(8,128)S(1)} %get-tuple-element.57.acc), custom_call_target="tpu_custom_call" | custom-call | bytes 12000000 | tf_op jit(solution)/shard_map/deposit/pallas_call | solution.py:446
  49.5 0.0 collective-permute-done.8.ymb
  49.5 0.0 collective-permute-done.9.yma
  49.6 1.0 %arrive.1 = f32[8,3,64,128]{3,2,1,0:T(8,128)} custom-call(f32[5,64,128]{2,1,0:T(8,128)S(1)} %collective-permute-done.4.ra, f32[5,64,128]{2,1,0:T(8,128)S(1)} %collective-permute-done.5.rb, f32[3,64,128]{2,1,0:T(8,128)S(1)} %collective-permute-done.6.yrb, f32[3,64,128]{2,1,0:T(8,128)S(1)} %collective-permute-done.7.yra, ...), custom_call_target="tpu_custom_call" | custom-call | bytes 3000000 | tf_op jit(solution)/shard_map/arrive/pallas_call | solution.py:450
  (9 shorter events, 0.0 us)
Async XLA Ops:
  3.1 23.3 %collective-permute-start = (f32[6,64,128]{2,1,0:T(8,128)S(1)}, f32[6,64,128]{2,1,0:T(8,128)S(1)}, u32[]{:S(2)}, u32[]{:S(2)}) collective-permute-start(f32[6,64,128]{2,1,0:T(8,128)S(1)} %get-tuple-element.36), channel_id=1, source_target_pairs={{0,248},{8,16},{16,8},{24,32},{32,24},{40,48},{48,40},{56,64},{64,... | collective-permute-start | bytes 589832 | tf_op jit(solution)/shard_map/ppermute | solution.py:400
  15.6 10.8 %collective-permute-start.1 = (f32[6,64,128]{2,1,0:T(8,128)S(1)}, f32[6,64,128]{2,1,0:T(8,128)S(1)}, u32[]{:S(2)}, u32[]{:S(2)}) collective-permute-start(f32[6,64,128]{2,1,0:T(8,128)S(1)} %get-tuple-element.37), channel_id=1, source_target_pairs={{0,8},{8,0},{16,24},{24,16},{32,40},{40,32},{48,56},{56,48},{64,72... | collective-permute-start | bytes 589832 | tf_op jit(solution)/shard_map/ppermute | solution.py:400
  15.6 10.8 %collective-permute-start.2 = (f32[2,32,128]{2,1,0:T(8,128)S(1)}, f32[2,32,128]{2,1,0:T(8,128)S(1)}, u32[]{:S(2)}, u32[]{:S(2)}) collective-permute-start(f32[2,32,128]{2,1,0:T(8,128)S(1)} %get-tuple-element.38), channel_id=1, source_target_pairs={{0,7},{1,2},{2,1},{3,4},{4,3},{5,6},{6,5},{7,0},{8,15},{9,10},{10,... | collective-permute-start | bytes 98312 | tf_op jit(solution)/shard_map/ppermute | solution.py:400
  17.1 9.2 %collective-permute-start.3 = (f32[2,32,128]{2,1,0:T(8,128)S(1)}, f32[2,32,128]{2,1,0:T(8,128)S(1)}, u32[]{:S(2)}, u32[]{:S(2)}) collective-permute-start(f32[2,32,128]{2,1,0:T(8,128)S(1)} %get-tuple-element.39), channel_id=1, source_target_pairs={{0,1},{1,0},{2,3},{3,2},{4,5},{5,4},{6,7},{7,6},{8,9},{9,8},{10,11... | collective-permute-start | bytes 98312 | tf_op jit(solution)/shard_map/ppermute | solution.py:400
  23.2 15.1 %copy-start = (s32[1,1,8,64]{3,2,1,0:T(8,128)S(1)}, s32[1,1,8,64]{3,2,1,0:T(8,128)}, u32[]{:S(2)}) copy-start(s32[1,1,8,64]{3,2,1,0:T(8,128)} %places.1) | copy-start | bytes 6148
  23.2 15.1 %copy-start.1 = (s32[2048]{0:T(1024)S(1)}, s32[2048]{0:T(1024)}, u32[]{:S(2)}) copy-start(s32[2048]{0:T(1024)} %home.1) | copy-start | bytes 24580
  23.2 15.1 %copy-start.2 = (s32[1,1,8]{2,1,0:T(1,128)S(1)}, s32[1,1,8]{2,1,0:T(1,128)}, u32[]{:S(2)}) copy-start(s32[1,1,8]{2,1,0:T(1,128)} %tallies.1) | copy-start | bytes 100
  28.0 17.0 %collective-permute-start.4 = (f32[5,64,128]{2,1,0:T(8,128)S(1)}, f32[5,64,128]{2,1,0:T(8,128)S(1)}, u32[]{:S(2)}, u32[]{:S(2)}) collective-permute-start(f32[5,64,128]{2,1,0:T(8,128)S(1)} %get-tuple-element.61), channel_id=1, source_target_pairs={{0,8},{8,0},{16,24},{24,16},{32,40},{40,32},{48,56},{56,48},{64,72... | collective-permute-start | bytes 491528 | tf_op jit(solution)/shard_map/ppermute | solution.py:400
  28.1 17.1 %collective-permute-start.5 = (f32[5,64,128]{2,1,0:T(8,128)S(1)}, f32[5,64,128]{2,1,0:T(8,128)S(1)}, u32[]{:S(2)}, u32[]{:S(2)}) collective-permute-start(f32[5,64,128]{2,1,0:T(8,128)S(1)} %get-tuple-element.62), channel_id=1, source_target_pairs={{0,248},{8,16},{16,8},{24,32},{32,24},{40,48},{48,40},{56,64},{64,... | collective-permute-start | bytes 491528 | tf_op jit(solution)/shard_map/ppermute | solution.py:400
  35.8 13.7 %collective-permute-start.8 = (f32[6,64,128]{2,1,0:T(8,128)S(1)}, f32[6,64,128]{2,1,0:T(8,128)S(1)}, u32[]{:S(2)}, u32[]{:S(2)}) collective-permute-start(f32[6,64,128]{2,1,0:T(8,128)S(1)} %get-tuple-element.66), channel_id=1, source_target_pairs={{0,7},{1,2},{2,1},{3,4},{4,3},{5,6},{6,5},{7,0},{8,15},{9,10},{10,... | collective-permute-start | bytes 589832 | tf_op jit(solution)/shard_map/ppermute | solution.py:400
  38.3 11.2 %collective-permute-start.9 = (f32[6,64,128]{2,1,0:T(8,128)S(1)}, f32[6,64,128]{2,1,0:T(8,128)S(1)}, u32[]{:S(2)}, u32[]{:S(2)}) collective-permute-start(f32[6,64,128]{2,1,0:T(8,128)S(1)} %get-tuple-element.67), channel_id=1, source_target_pairs={{0,1},{1,0},{2,3},{3,2},{4,5},{5,4},{6,7},{7,6},{8,9},{9,8},{10,11... | collective-permute-start | bytes 589832 | tf_op jit(solution)/shard_map/ppermute | solution.py:400
  45.3 4.3 %collective-permute-start.6 = (f32[3,64,128]{2,1,0:T(8,128)S(1)}, f32[3,64,128]{2,1,0:T(8,128)S(1)}, u32[]{:S(2)}, u32[]{:S(2)}) collective-permute-start(f32[3,64,128]{2,1,0:T(8,128)S(1)} %get-tuple-element.64), channel_id=1, source_target_pairs={{0,7},{1,2},{2,1},{3,4},{4,3},{5,6},{6,5},{7,0},{8,15},{9,10},{10,... | collective-permute-start | bytes 294920 | tf_op jit(solution)/shard_map/ppermute | solution.py:400
  45.4 4.2 %collective-permute-start.7 = (f32[3,64,128]{2,1,0:T(8,128)S(1)}, f32[3,64,128]{2,1,0:T(8,128)S(1)}, u32[]{:S(2)}, u32[]{:S(2)}) collective-permute-start(f32[3,64,128]{2,1,0:T(8,128)S(1)} %get-tuple-element.65), channel_id=1, source_target_pairs={{0,1},{1,0},{2,3},{3,2},{4,5},{5,4},{6,7},{7,6},{8,9},{9,8},{10,11... | collective-permute-start | bytes 294920 | tf_op jit(solution)/shard_map/ppermute | solution.py:400
